TPU v7x, 32 devices: a whole 2x2x4 slice. The times are simulated.
32 devices in a mesh: src: 4 (over z), tgt: 8 (over y, x, core).
Axes of the slice: x: 2, y: 2, z: 4, core: 2. Of those that a mesh axis runs over, the one named last changes fastest.
Arguments:
- src_points: bfloat16 [32, 256, 128], P('src', 'tgt')
- tgt_points: bfloat16 [64, 256, 128], P('tgt', 'src'), may hold values from -1.5 to 1.5
- src_mass: bfloat16 [32, 256], P('src', 'tgt'), may hold values from 0.099609375 to 10
- tgt_mass: bfloat16 [64, 256], P('tgt', 'src'), may hold values from 0.099609375 to 10
- src_potential: bfloat16 [32, 256], P('src', 'tgt'), may hold values from -452 to 452
- tgt_potential: bfloat16 [64, 256], P('tgt', 'src'), may hold values from -452 to 452
- src_counts: int32 [32], P('src'), may hold values from 16 to 256, as said below
- tgt_counts: int32 [64], P('tgt'), may hold values from 16 to 256, as said below
- keep: int32 [32, 64], P('src', 'tgt'), may hold values from 0 to 1, as said below
Outputs:
- images: float32 [32, 256, 128], P('src', 'tgt')
- src_final: float32 [32, 256], P('src', 'tgt')
- tgt_final: float32 [64, 256], P('tgt', 'src')
Inputs may be any that keep to these rules, and one draw needn't show every extreme that they name: `keep`: every source block keeps at least one target block and every target block is kept by at least one source block. `src_counts`: some source block is full. `tgt_counts`: some target block is full.
All inputs are finite; a program needn't handle non-finite values.
Results may differ from a plain program's by a relative error of at most 0.0003.
Values may be sent and summed in bfloat16 or wider, within the bound.
No kernel may reach another device: no remote copies, remote signals or barrier semaphores. Data moves between devices by JAX's collectives and lax.ppermute only.
A program may use at most 64 MiB of HBM per device.

v0:
```python
import jax
import jax.numpy as jnp
from jax import lax
from jax.sharding import PartitionSpec as P

ITERS = 4


EPSILON = 0.1
FLOOR = -1e30


def merged(shard, axis, combine):
    everything = jax.tree.map(lambda part: lax.all_gather(part, axis), shard)
    leading = jax.tree.map(lambda part: part[0], everything)

    def lap(k, so_far):
        return combine(so_far, jax.tree.map(lambda part: part[k], everything))

    return lax.fori_loop(1, lax.axis_size(axis), lap, leading)


def merge_triple(first, second):
    peak = jnp.maximum(first[0], second[0])
    scale_a = jnp.exp(first[0] - peak)
    scale_b = jnp.exp(second[0] - peak)
    return (
        peak,
        first[1] * scale_a + second[1] * scale_b,
        first[2] * scale_a[:, None] + second[2] * scale_b[:, None],
    )


def row_lse(peak, total):
    top = lax.pmax(peak, "tgt")
    whole = (top, lax.psum(total * jnp.exp(peak - top), "tgt"))
    return whole


def col_lse(peak, total):
    top = lax.pmax(peak, "src")
    whole = (top, lax.psum(total * jnp.exp(peak - top), "src"))
    return whole


def on_device(
    src_points,
    tgt_points,
    src_mass,
    tgt_mass,
    src_potential,
    tgt_potential,
    src_counts,
    tgt_counts,
    keep,
):
    xs_all, a_mass, f_start = (
        lax.all_gather(src_points, "tgt", axis=1, tiled=True),
        lax.all_gather(src_mass, "tgt", axis=1, tiled=True),
        lax.all_gather(src_potential, "tgt", axis=1, tiled=True),
    )
    ys_all, b_mass, g_start = (
        lax.all_gather(tgt_points, "src", axis=1, tiled=True),
        lax.all_gather(tgt_mass, "src", axis=1, tiled=True),
        lax.all_gather(tgt_potential, "src", axis=1, tiled=True),
    )
    sb, blk, width = xs_all.shape
    tb = ys_all.shape[0]
    ncols = tb * blk
    group = min(sb, max(1, 512 // blk))
    steps_n = sb // group
    rows = group * blk
    x_flat = xs_all.reshape(sb * blk, width)
    y_flat = ys_all.reshape(ncols, width)
    x_wide = x_flat.astype(jnp.float32)
    y_wide = y_flat.astype(jnp.float32)
    x_half = (0.5 * jnp.sum(x_wide * x_wide, axis=1)).reshape(steps_n, rows)
    y_half = 0.5 * jnp.sum(y_wide * y_wide, axis=1)
    slots = jnp.arange(blk, dtype=jnp.int32)
    src_live = (slots[None, :] < src_counts[:, None]).reshape(steps_n, rows)
    tgt_live = (slots[None, :] < tgt_counts[:, None]).reshape(-1)
    log_a = jnp.log(a_mass.astype(jnp.float32)).reshape(steps_n, rows)
    log_b = jnp.log(b_mass.astype(jnp.float32)).reshape(-1)
    keep_grp = jnp.repeat(keep > 0, blk, axis=1).reshape(steps_n, group, ncols)
    x_grp = x_flat.reshape(steps_n, rows, width)

    def tile(x, xh, blocks):
        cost = (
            xh[:, None]
            + y_half[None, :]
            - lax.dot_general(
                x, y_flat, (((1,), (1,)), ((), ())), preferred_element_type=jnp.float32
            )
        )
        return (cost, jnp.repeat(blocks, blk, axis=0))

    def row_scores(cost, pair, g_now):
        row_ok = pair & tgt_live[None, :]
        scored = jnp.where(row_ok, log_b[None, :] + (g_now[None, :] - cost) / EPSILON, FLOOR)
        return (scored, row_ok)

    def local_rows(scored, row_ok):
        peak = jnp.max(scored, axis=1)
        weights = jnp.where(row_ok, jnp.exp(scored - peak[:, None]), 0.0)
        return (peak, weights)

    f_cur = f_start.astype(jnp.float32).reshape(-1)
    g_cur = g_start.astype(jnp.float32).reshape(-1)
    for step in range(ITERS):
        sweep_g_now = g_cur

        def visit(carry, item):
            colmax, colsum = carry
            x, xh, live, lga, fpart, blocks = item
            cost, pair = tile(x, xh, blocks)
            scored, row_ok = row_scores(cost, pair, sweep_g_now)
            peak, weights = local_rows(scored, row_ok)
            col_ok = pair & live[:, None]
            colterm = jnp.where(col_ok, lga[:, None] + (fpart[:, None] - cost) / EPSILON, FLOOR)
            top = jnp.maximum(colmax, jnp.max(colterm, axis=0))
            colsum = colsum * jnp.exp(colmax - top) + jnp.sum(
                jnp.where(col_ok, jnp.exp(colterm - top[None, :]), 0.0), axis=0
            )
            return ((top, colsum), (peak, jnp.sum(weights, axis=1)))

        start = (jnp.full((ncols,), FLOOR, jnp.float32), jnp.zeros((ncols,), jnp.float32))
        (colmax, colsum), (rpeak, rtotal) = lax.scan(
            visit, start, (x_grp, x_half, src_live, log_a, f_cur.reshape(steps_n, rows), keep_grp)
        )
        whole_rows = row_lse(rpeak.reshape(-1), rtotal.reshape(-1))
        whole_cols = col_lse(colmax, colsum)
        f_new = -EPSILON * (whole_rows[0] + jnp.log(whole_rows[1]))
        g_new = -EPSILON * (whole_cols[0] + jnp.log(whole_cols[1]))
        f_new, g_new = (f_new, g_new)
        f_cur = 0.5 * (f_cur + f_new)
        g_cur = 0.5 * (g_cur + g_new)
    ntgt = lax.axis_size("tgt")
    nsrc = lax.axis_size("src")
    src_piece = blk // ntgt
    tgt_piece = blk // nsrc
    src_start = lax.axis_index("tgt") * src_piece
    tgt_start = lax.axis_index("src") * tgt_piece

    def project_local(carry, item):
        x, xh, blocks = item
        cost, pair = tile(x, xh, blocks)
        scored, row_ok = row_scores(cost, pair, g_cur)
        peak, weights = local_rows(scored, row_ok)
        moved = jnp.dot(weights, y_wide, precision=lax.Precision.HIGHEST)
        return (carry, (peak, jnp.sum(weights, axis=1), moved))

    unused, (peak, total, moved) = lax.scan(
        project_local, jnp.zeros((), jnp.float32), (x_grp, x_half, keep_grp)
    )
    whole = merged(
        (peak.reshape(-1), total.reshape(-1), moved.reshape(sb * blk, width)), "tgt", merge_triple
    )
    mapped = (whole[2] / whole[1][:, None]).reshape(sb, blk, width)
    images = lax.dynamic_slice_in_dim(mapped, src_start, src_piece, 1)
    src_final = lax.dynamic_slice_in_dim(f_cur.reshape(sb, blk), src_start, src_piece, 1)
    tgt_final = lax.dynamic_slice_in_dim(g_cur.reshape(tb, blk), tgt_start, tgt_piece, 1)
    return (images, src_final, tgt_final)


def solution(mesh):
    return jax.shard_map(
        on_device,
        mesh=mesh,
        in_specs=(
            P("src", "tgt", None),
            P("tgt", "src", None),
            P("src", "tgt"),
            P("tgt", "src"),
            P("src", "tgt"),
            P("tgt", "src"),
            P("src"),
            P("tgt"),
            P("src", "tgt"),
        ),
        out_specs=(P("src", "tgt", None), P("src", "tgt"), P("tgt", "src")),
        check_vma=False,
    )
```

profile of v0, /device:TPU:0, one launch (start us, length us, event | category | flops | bytes accessed | tf_op | source)
XLA Modules:
  0.0 488.6 jit_solution(13918108128651018545)
XLA Ops:
  7.3 17.6 %all_gather.32 = bf16[8,256,128]{2,1,0:T(8,128)(2,1)S(1)} all-gather(bf16[8,64,128]{2,1,0:T(8,128)(2,1)} %param.22), channel_id=1, replica_groups=mesh['src'=4,'tgt'=8] {'src'}, dimensions={1}, use_global_device_ids=true | all-gather | bytes 655360 | tf_op jit(solution)/shard_map/all_gather | solution.py:63
  25.4 10.2 %all_gather.31 = bf16[8,256,128]{2,1,0:T(8,128)(2,1)S(1)} all-gather(bf16[8,32,128]{2,1,0:T(8,128)(2,1)} %param.21), channel_id=1, replica_groups=mesh['src'=4,'tgt'=8] {'tgt'}, dimensions={1}, use_global_device_ids=true | all-gather | bytes 589824 | tf_op jit(solution)/shard_map/all_gather | solution.py:58
  36.7 12.4 %all-gather = bf16[4,64,8]{1,2,0:T(8,128)(2,1)S(1)} all-gather(bf16[1,64,8]{1,2,0:T(8,128)(2,1)} %bitcast.475), channel_id=1, replica_groups=mesh['src'=4,'tgt'=8] {'src'}, dimensions={0}, use_global_device_ids=true | all-gather | bytes 5120 | tf_op jit(solution)/shard_map/all_gather | solution.py:64
  66.4 11.9 %all-gather.1 = bf16[4,64,8]{1,2,0:T(8,128)(2,1)S(1)} all-gather(bf16[1,64,8]{1,2,0:T(8,128)(2,1)S(1)} %bitcast.478), channel_id=1, replica_groups=mesh['src'=4,'tgt'=8] {'src'}, dimensions={0}, use_global_device_ids=true | all-gather | bytes 5120 | tf_op jit(solution)/shard_map/all_gather | solution.py:65
  78.4 39.3 %while.104 = (s32[]{:T(128)}, f32[2048]{0:T(1024)S(1)}, f32[2048]{0:T(1024)S(1)}, f32[4,512]{1,0:T(4,128)S(1)}, f32[4,512]{1,0:T(4,128)S(1)}, /*index=5*/pred[4,...) while((s32[]{:T(128)}, f32[2048]{0:T(1024)S(1)}, ...), condition=%wide.region_7.8_spmd.clone, body=%wide.region_2.7_spmd.clone.sunk | while | flops 302001152 | bytes 9304300 | solution.py:127
  117.7 12.0 %pmax.57 = f32[2048]{0:T(1024)S(1)} all-reduce(f32[2048]{0:T(1024)S(1)} %bitcast.452), channel_id=1, replica_groups=mesh['src'=4,'tgt'=8] {'tgt'}, use_global_device_ids=true, to_apply=%region_10.11 | all-reduce | flops 2048 | bytes 16384 | tf_op jit(solution)/shard_map/pmax | solution.py:35
  129.8 12.0 %psum.57 = f32[2048]{0:T(1024)S(1)} all-reduce(f32[2048]{0:T(1024)S(1)} %exponential_multiply_fusion.6), channel_id=1, replica_groups=mesh['src'=4,'tgt'=8] {'tgt'}, use_global_device_ids=true, to_apply=%region_11.12 | all-reduce | flops 2048 | bytes 16384 | tf_op jit(solution)/shard_map/psum | solution.py:36
  141.9 9.7 %pmax.56 = f32[2048]{0:T(1024)S(1)} all-reduce(f32[2048]{0:T(1024)S(1)} %get-tuple-element.589), channel_id=1, replica_groups=mesh['src'=4,'tgt'=8] {'src'}, use_global_device_ids=true, to_apply=%region_8.9 | all-reduce | flops 2048 | bytes 16384 | tf_op jit(solution)/shard_map/pmax | solution.py:41
  161.0 39.2 %while.105 = (s32[]{:T(128)}, f32[2048]{0:T(1024)S(1)}, f32[2048]{0:T(1024)S(1)}, f32[4,512]{1,0:T(4,128)S(1)}, f32[4,512]{1,0:T(4,128)S(1)}, /*index=5*/pred[4,...) while((s32[]{:T(128)}, f32[2048]{0:T(1024)S(1)}, ...), condition=%wide.region_17.18_spmd.clone, body=%wide.region_12.17_spmd.clone.sunk | while | flops 302001152 | bytes 9287916 | solution.py:127
  200.2 12.0 %pmax.59 = f32[2048]{0:T(1024)S(1)} all-reduce(f32[2048]{0:T(1024)S(1)} %bitcast.454), channel_id=1, replica_groups=mesh['src'=4,'tgt'=8] {'tgt'}, use_global_device_ids=true, to_apply=%region_20.21 | all-reduce | flops 2048 | bytes 16384 | tf_op jit(solution)/shard_map/pmax | solution.py:35
  212.3 12.0 %psum.59 = f32[2048]{0:T(1024)S(1)} all-reduce(f32[2048]{0:T(1024)S(1)} %exponential_multiply_fusion.4), channel_id=1, replica_groups=mesh['src'=4,'tgt'=8] {'tgt'}, use_global_device_ids=true, to_apply=%region_21.22 | all-reduce | flops 2048 | bytes 16384 | tf_op jit(solution)/shard_map/psum | solution.py:36
  224.4 9.7 %pmax.58 = f32[2048]{0:T(1024)S(1)} all-reduce(f32[2048]{0:T(1024)S(1)} %get-tuple-element.593), channel_id=1, replica_groups=mesh['src'=4,'tgt'=8] {'src'}, use_global_device_ids=true, to_apply=%region_18.19 | all-reduce | flops 2048 | bytes 16384 | tf_op jit(solution)/shard_map/pmax | solution.py:41
  234.2 9.5 %psum.58 = f32[2048]{0:T(1024)S(1)} all-reduce(f32[2048]{0:T(1024)S(1)} %exponential_multiply_fusion.5), channel_id=1, replica_groups=mesh['src'=4,'tgt'=8] {'src'}, use_global_device_ids=true, to_apply=%region_19.20 | all-reduce | flops 2048 | bytes 16384 | tf_op jit(solution)/shard_map/psum | solution.py:42
  243.7 39.1 %while.106 = (s32[]{:T(128)}, f32[2048]{0:T(1024)S(1)}, f32[2048]{0:T(1024)S(1)}, f32[4,512]{1,0:T(4,128)S(1)}, f32[4,512]{1,0:T(4,128)S(1)}, /*index=5*/pred[4,...) while((s32[]{:T(128)}, f32[2048]{0:T(1024)S(1)}, ...), condition=%wide.region_27.28_spmd.clone, body=%wide.region_22.27_spmd.clone.sunk | while | flops 302001152 | bytes 9287916 | solution.py:127
  282.8 12.0 %pmax.61 = f32[2048]{0:T(1024)S(1)} all-reduce(f32[2048]{0:T(1024)S(1)} %bitcast.456), channel_id=1, replica_groups=mesh['src'=4,'tgt'=8] {'tgt'}, use_global_device_ids=true, to_apply=%region_30.31 | all-reduce | flops 2048 | bytes 16384 | tf_op jit(solution)/shard_map/pmax | solution.py:35
  294.9 12.0 %psum.61 = f32[2048]{0:T(1024)S(1)} all-reduce(f32[2048]{0:T(1024)S(1)} %exponential_multiply_fusion.2), channel_id=1, replica_groups=mesh['src'=4,'tgt'=8] {'tgt'}, use_global_device_ids=true, to_apply=%region_31.32 | all-reduce | flops 2048 | bytes 16384 | tf_op jit(solution)/shard_map/psum | solution.py:36
  307.0 9.7 %pmax.60 = f32[2048]{0:T(1024)S(1)} all-reduce(f32[2048]{0:T(1024)S(1)} %get-tuple-element.597), channel_id=1, replica_groups=mesh['src'=4,'tgt'=8] {'src'}, use_global_device_ids=true, to_apply=%region_28.29 | all-reduce | flops 2048 | bytes 16384 | tf_op jit(solution)/shard_map/pmax | solution.py:41
  326.1 39.2 %while.107 = (s32[]{:T(128)}, f32[2048]{0:T(1024)S(1)}, f32[2048]{0:T(1024)S(1)}, f32[4,512]{1,0:T(4,128)S(1)}, f32[4,512]{1,0:T(4,128)S(1)}, /*index=5*/pred[4,...) while((s32[]{:T(128)}, f32[2048]{0:T(1024)S(1)}, ...), condition=%wide.region_37.38_spmd.clone, body=%wide.region_32.37_spmd.clone.sunk | while | flops 302001152 | bytes 9287916 | solution.py:127
  365.3 9.7 %pmax.62 = f32[2048]{0:T(1024)S(1)} all-reduce(f32[2048]{0:T(1024)S(1)} %get-tuple-element.601), channel_id=1, replica_groups=mesh['src'=4,'tgt'=8] {'src'}, use_global_device_ids=true, to_apply=%region_38.39 | all-reduce | flops 2048 | bytes 16384 | tf_op jit(solution)/shard_map/pmax | solution.py:41
  375.1 9.5 %psum.62 = f32[2048]{0:T(1024)S(1)} all-reduce(f32[2048]{0:T(1024)S(1)} %exponential_multiply_fusion.1), channel_id=1, replica_groups=mesh['src'=4,'tgt'=8] {'src'}, use_global_device_ids=true, to_apply=%region_39.40 | all-reduce | flops 2048 | bytes 16384 | tf_op jit(solution)/shard_map/psum | solution.py:42
  384.7 26.2 %while.103 = (s32[]{:T(128)}, f32[4,512]{1,0:T(4,128)S(1)}, f32[4,512]{1,0:T(4,128)S(1)}, f32[4,512,128]{2,1,0:T(8,128)}, pred[4,2,2048]{2,1,0:T(4,128)(4,1)S(1)...) while((s32[]{:T(128)}, f32[4,512]{1,0:T(4,128)S(1)}, ...), condition=%wide.region_43.44_spmd.clone, body=%wide.region_40.43_spmd.clone.sunk | while | flops 1891632128 | bytes 18836160 | solution.py:152
  428.6 13.6 %pmax.63 = f32[2048]{0:T(1024)S(1)} all-reduce(f32[2048]{0:T(1024)S(1)} %bitcast.450), channel_id=1, replica_groups=mesh['src'=4,'tgt'=8] {'tgt'}, use_global_device_ids=true, to_apply=%region_46.47 | all-reduce | flops 2048 | bytes 16384 | tf_op jit(solution)/shard_map/pmax | solution.py:35
  442.3 12.7 %psum.63 = f32[2048]{0:T(1024)S(1)} all-reduce(f32[2048]{0:T(1024)S(1)} %exponential_multiply_fusion), channel_id=1, replica_groups=mesh['src'=4,'tgt'=8] {'tgt'}, use_global_device_ids=true, to_apply=%region_47.48 | all-reduce | flops 2048 | bytes 16384 | tf_op jit(solution)/shard_map/psum | solution.py:36
  465.6 15.1 %while.102 = (s32[]{:T(128)}, f32[2048]{0:T(1024)S(1)}, f32[2048]{0:T(1024)S(1)}, f32[2048,128]{1,0:T(8,128)S(1)}, f32[8,2048]{1,0:T(8,128)S(1)}, /*index=5*/f32...) while((s32[]{:T(128)}, f32[2048]{0:T(1024)S(1)}, f32[2048]{0:T(1024)S(1)}, ...), condition=%wide.region_45.46_spmd, body=%wide.region_44.45_spmd.sunk | while | flops 798725 | bytes 3260567 | solution.py:20
  (395 shorter events, 263.6 us)
Async XLA Ops:
  7.2 50.8 %copy-start.3 = (s32[8]{0:T(128)S(1)}, s32[8]{0:T(128)}, u32[]{:S(2)}) copy-start(s32[8]{0:T(128)} %param.27) | copy-start | bytes 100
  7.2 50.9 %copy-start.1 = (bf16[8,32]{1,0:T(8,128)(2,1)S(1)}, bf16[8,32]{1,0:T(8,128)(2,1)}, u32[]{:S(2)}) copy-start(bf16[8,32]{1,0:T(8,128)(2,1)} %param.25) | copy-start | bytes 1540
  7.2 59.2 %copy-start.2 = (bf16[8,64]{1,0:T(8,128)(2,1)S(1)}, bf16[8,64]{1,0:T(8,128)(2,1)}, u32[]{:S(2)}) copy-start(bf16[8,64]{1,0:T(8,128)(2,1)} %param.26) | copy-start | bytes 3076
  7.2 71.2 %copy-start = (s32[8]{0:T(128)S(1)}, s32[8]{0:T(128)}, u32[]{:S(2)}) copy-start(s32[8]{0:T(128)} %param.28) | copy-start | bytes 100
  7.2 457.1 %all-gather.8.cloned.1.call-start = ((), (), s32[]{:S(2)}) async-start(), calls=%async_computation | async-start | bytes 9437184 | tf_op jit(solution)/shard_map/all_gather | solution.py:14
Sparse Core Ops, SparseCore 0:
  411.1 53.1 all-gather.7
where the time goes:
time: 490 us; the launch traced here: 489 us
  blocking collectives  262 us (53%)
  other arithmetic  112 us (23%)
  matrix products  83 us (17%)
  between operations  14.8 us (3%)
  waiting for transfers between devices  7.94 us (2%)
  local copies, waits for them, and re-layouts  7.8 us (2%)
    reduce_sum x16, other arithmetic, visit(): return ((top, colsum), (peak, jnp.sum(weights, axis=1)))  90 us
    dot_general x20, matrix products, tile(): lax.dot_general(x, y_flat, (((1,), (1,)), ((), ())), preferred_element_ty...  66.4 us
    pmax x4, blocking collectives, row_lse(): top = lax.pmax(peak, 'tgt')  49.8 us
    psum x4, blocking collectives, row_lse(): whole = (top, lax.psum(total * jnp.exp(peak - top), 'tgt'))  48.9 us
    pmax x4, blocking collectives, col_lse(): top = lax.pmax(peak, 'src')  39 us
    psum x4, blocking collectives, col_lse(): whole = (top, lax.psum(total * jnp.exp(peak - top), 'src'))  37.6 us
    all_gather x1, blocking collectives, on_device(): lax.all_gather(tgt_points, 'src', axis=1, tiled=True)  17.6 us
    all_gather x2, blocking collectives, merged(): everything = jax.tree.map(lambda part: lax.all_gather(part, axis), shard)  17.5 us
  transfers between devices with their start and end apart: 1, of which 1 were waited for; matrix products, arithmetic and copies ran while one was open for 0% of the time, Pallas kernels for 0%

commit v1 on v0

v1 whole, which is shorter than its diff:
```python
import functools
import math

import jax
import jax.numpy as jnp
from jax import lax
from jax.experimental import pallas as pl
from jax.experimental.pallas import tpu as pltpu
from jax.sharding import PartitionSpec as P

ITERS = 4
EPSILON = 0.1
UNIT = 1.0 / (EPSILON * math.log(2.0))
FLOOR = -1e30


def whole_block(ref, k):
    piece = ref[:, k]
    return piece.reshape(piece.shape[0] * piece.shape[1], piece.shape[2])


def spread_columns(vec, col_ref):
    turned = vec.T
    for k in range(vec.shape[0]):
        col_ref[k] = jnp.broadcast_to(turned[:, k : k + 1], col_ref.shape[1:])


def reduce_pass(lane_ref, lane_blocks, stream_ref, stream_blocks, col_ref, kept, peak_ref, sum_ref):
    peak_ref[...] = jnp.full(peak_ref.shape, FLOOR, jnp.float32)
    sum_ref[...] = jnp.zeros(sum_ref.shape, jnp.float32)

    @pl.loop(0, lane_blocks)
    def _(p):
        @pl.loop(0, stream_blocks)
        def _(q):
            @pl.when(kept(p, q))
            def _():
                dots = lax.dot_general(
                    whole_block(stream_ref, q),
                    whole_block(lane_ref, p),
                    (((1,), (1,)), ((), ())),
                    preferred_element_type=jnp.float32,
                )
                n, lanes = dots.shape
                col = col_ref[q]
                col = jnp.concatenate([col] * (lanes // 128), axis=1)
                score = (dots * UNIT + col).reshape(n // 8, 8, lanes)
                old = peak_ref[p]
                new = jnp.maximum(old, jnp.max(score, axis=0))
                sum_ref[p] = sum_ref[p] * jnp.exp2(old - new) + jnp.sum(jnp.exp2(score - new[None]), axis=0)
                peak_ref[p] = new

    peak = peak_ref[...]
    top = jnp.max(peak, axis=1, keepdims=True)
    total = jnp.sum(sum_ref[...] * jnp.exp2(peak - top), axis=1)
    return top[:, 0] + jnp.log2(total)


def sweep_kernel(keep_ref, x_ref, y_ref, u_ref, h_ref, rows_ref, cols_ref, col_ref, peak_ref, sum_ref):
    sb, tb = x_ref.shape[1], y_ref.shape[1]
    spread_columns(h_ref[...], col_ref)
    rows_ref[...] = reduce_pass(
        x_ref, sb, y_ref, tb, col_ref, lambda p, q: keep_ref[p, q] > 0, peak_ref, sum_ref
    )
    spread_columns(u_ref[...], col_ref)
    cols_ref[...] = reduce_pass(
        y_ref, tb, x_ref, sb, col_ref, lambda q, p: keep_ref[p, q] > 0, peak_ref, sum_ref
    )


def project_kernel(keep_ref, x_ref, y_ref, h_ref, image_ref, lse_ref, acc_ref, peak_ref):
    sb, tb = x_ref.shape[1], y_ref.shape[1]
    width = x_ref.shape[3]

    @pl.loop(0, sb)
    def _(p):
        acc_ref[...] = jnp.zeros(acc_ref.shape, jnp.float32)
        peak_ref[...] = jnp.full(peak_ref.shape, FLOOR, jnp.float32)

        @pl.loop(0, tb)
        def _(q):
            @pl.when(keep_ref[p, q] > 0)
            def _():
                ys = whole_block(y_ref, q)
                dots = lax.dot_general(
                    whole_block(x_ref, p), ys, (((1,), (1,)), ((), ())), preferred_element_type=jnp.float32
                )
                score = dots * UNIT + h_ref[pl.ds(q, 1), :]
                old = peak_ref[...]
                new = jnp.maximum(old, jnp.max(score, axis=1, keepdims=True))
                weights = jnp.exp2(score - new[:, :1])
                high = weights.astype(jnp.bfloat16)
                low = (weights - high.astype(jnp.float32)).astype(jnp.bfloat16)
                full = jnp.concatenate([ys, jnp.ones(ys.shape, ys.dtype)], axis=1)
                moved = jnp.dot(high, full, preferred_element_type=jnp.float32) + jnp.dot(
                    low, full, preferred_element_type=jnp.float32
                )
                acc_ref[...] = acc_ref[...] * jnp.exp2(old - new)[:, :1] + moved
                peak_ref[...] = new

        total = acc_ref[:, width:]
        safe = jnp.where(total > 0.0, total, 1.0)
        image_ref[p] = acc_ref[:, :width] / safe
        lse = peak_ref[...] + jnp.log2(safe)
        lse_ref[pl.ds(p, 1), :] = lse.T[:1]


def merge_lse(parts):
    top = functools.reduce(jnp.maximum, parts)
    return top + jnp.log2(sum(jnp.exp2(part - top) for part in parts))


def all_lse(part, axis):
    got = lax.all_gather(part, axis)
    return merge_lse([got[k] for k in range(got.shape[0])])


def on_device(
    src_points, tgt_points, src_mass, tgt_mass, src_potential, tgt_potential, src_counts, tgt_counts, keep
):
    ntgt = lax.axis_size("tgt")
    nsrc = lax.axis_size("src")
    sb, src_piece, width = src_points.shape
    tb, tgt_piece, _ = tgt_points.shape
    blk = src_piece * ntgt

    x = lax.all_gather(src_points, "tgt")
    y = lax.all_gather(tgt_points, "src")

    def vectors(mass, potential, points, counts, axis):
        pair = lax.all_gather(jnp.stack([mass, potential]), axis).astype(jnp.float32)
        pair = jnp.transpose(pair, (1, 2, 0, 3)).reshape(2, mass.shape[0], blk)
        wide = points.astype(jnp.float32)
        half = jnp.transpose((0.5 * UNIT) * jnp.sum(wide * wide, axis=3), (1, 0, 2)).reshape(mass.shape[0], blk)
        live = jnp.arange(blk, dtype=jnp.int32)[None, :] < counts[:, None]
        return pair[1] * UNIT, half, jnp.log2(pair[0]) - half, live

    f, x_half, x_base, src_live = vectors(src_mass, src_potential, x, src_counts, "tgt")
    g, y_half, y_base, tgt_live = vectors(tgt_mass, tgt_potential, y, tgt_counts, "src")

    smem = pl.BlockSpec(memory_space=pltpu.SMEM)
    vmem = pl.BlockSpec(memory_space=pltpu.VMEM)
    most = max(sb, tb)
    params = pltpu.CompilerParams(vmem_limit_bytes=40 * 1024 * 1024)
    sweep = pl.pallas_call(
        sweep_kernel,
        out_shape=(jax.ShapeDtypeStruct((sb, blk), jnp.float32), jax.ShapeDtypeStruct((tb, blk), jnp.float32)),
        in_specs=[smem] + [vmem] * 4,
        out_specs=(vmem, vmem),
        scratch_shapes=[
            pltpu.VMEM((most, blk, 128), jnp.float32),
            pltpu.VMEM((most, 8, blk), jnp.float32),
            pltpu.VMEM((most, 8, blk), jnp.float32),
        ],
        compiler_params=params,
        name="sweep",
    )
    project = pl.pallas_call(
        project_kernel,
        out_shape=(
            jax.ShapeDtypeStruct((sb, blk, width), jnp.float32),
            jax.ShapeDtypeStruct((sb, blk), jnp.float32),
        ),
        in_specs=[smem] + [vmem] * 3,
        out_specs=(vmem, vmem),
        scratch_shapes=[pltpu.VMEM((blk, 2 * width), jnp.float32), pltpu.VMEM((blk, 128), jnp.float32)],
        compiler_params=params,
        name="project",
    )

    for step in range(ITERS):
        u = jnp.where(src_live, f + x_base, FLOOR)
        h = jnp.where(tgt_live, g + y_base, FLOOR)
        rows, cols = sweep(keep, x, y, u, h)
        rows = all_lse(rows, "tgt")
        cols = all_lse(cols, "src")
        f = 0.5 * (f + (x_half - rows))
        g = 0.5 * (g + (y_half - cols))

    h = jnp.where(tgt_live, g + y_base, FLOOR)
    image, lse = project(keep, x, y, h)
    whole = all_lse(lse, "tgt")
    image = image * jnp.exp2(lse - whole)[:, :, None]
    pieces = lax.all_to_all(image.reshape(sb, ntgt, src_piece, width), "tgt", 1, 0)
    images = jnp.sum(pieces, axis=0)
    src_start = lax.axis_index("tgt") * src_piece
    tgt_start = lax.axis_index("src") * tgt_piece
    src_final = lax.dynamic_slice_in_dim(f * (1.0 / UNIT), src_start, src_piece, 1)
    tgt_final = lax.dynamic_slice_in_dim(g * (1.0 / UNIT), tgt_start, tgt_piece, 1)
    return images, src_final, tgt_final


def solution(mesh):
    return jax.shard_map(
        on_device,
        mesh=mesh,
        in_specs=(
            P("src", "tgt", None),
            P("tgt", "src", None),
            P("src", "tgt"),
            P("tgt", "src"),
            P("src", "tgt"),
            P("tgt", "src"),
            P("src"),
            P("tgt"),
            P("src", "tgt"),
        ),
        out_specs=(P("src", "tgt", None), P("src", "tgt"), P("tgt", "src")),
        check_vma=False,
    )
```

time: 490 us -> 244 us (0.50)
  the two profiles are of different devices: /device:TPU:0 before, /device:TPU:25 now
where the time goes in v1:
time: 244 us; the launch traced here: 242 us
  blocking collectives  175 us (72%)
  Pallas kernels  53.1 us (22%)
  local copies, waits for them, and re-layouts  5.44 us (2%)
  other arithmetic  3.85 us (2%)
  starting transfers between devices  3.64 us (1%)
    all_gather x9, blocking collectives, all_lse(): got = lax.all_gather(part, axis)  133 us
    pallas_call x4, Pallas kernels, on_device(): rows, cols = sweep(keep, x, y, u, h)  41.7 us
    all_gather x2, blocking collectives, vectors(): lax.all_gather(jnp.stack([mass, potential]), axis).astype(jnp.float32)  18.9 us
    all_gather x1, blocking collectives, on_device(): y = lax.all_gather(tgt_points, 'src')  13.1 us
    pallas_call x1, Pallas kernels, on_device(): image, lse = project(keep, x, y, h)  11.4 us
    all_gather x1, blocking collectives, on_device(): x = lax.all_gather(src_points, 'tgt')  10.7 us
  transfers between devices with their start and end apart: 1, of which 0 were waited for; matrix products, arithmetic and copies ran while one was open for 1% of the time, Pallas kernels for 0%

profile of v1, /device:TPU:25, one launch (start us, length us, event | category | flops | bytes accessed | tf_op | source)
XLA Modules:
  0.0 242.2 jit_solution(16167922619066288989)
XLA Ops:
  0.6 10.7 %all-gather = bf16[64,32,128]{2,1,0:T(8,128)(2,1)S(1)} all-gather(bf16[8,32,128]{2,1,0:T(8,128)(2,1)} %param.9), channel_id=2, replica_groups=mesh['src'=4,'tgt'=8] {'tgt'}, dimensions={0}, use_global_device_ids=true | all-gather | bytes 589824 | tf_op jit(solution)/shard_map/all_gather | solution.py:127
  12.5 8.7 %all-gather.3 = bf16[16,8,32]{2,1,0:T(8,128)(2,1)S(1)} all-gather(bf16[2,8,32]{2,1,0:T(8,128)(2,1)S(1)} %pad_maximum_fusion.1), channel_id=5, replica_groups=mesh['src'=4,'tgt'=8] {'tgt'}, dimensions={0}, use_global_device_ids=true | all-gather | bytes 9216 | tf_op jit(solution)/shard_map/all_gather | solution.py:131
  21.4 0.7 copy-done.1
  22.1 13.1 %all-gather.1 = bf16[32,64,128]{2,1,0:T(8,128)(2,1)S(1)} all-gather(bf16[8,64,128]{2,1,0:T(8,128)(2,1)S(1)} %copy-done.1), channel_id=3, replica_groups=mesh['src'=4,'tgt'=8] {'src'}, dimensions={0}, use_global_device_ids=true | all-gather | bytes 655360 | tf_op jit(solution)/shard_map/all_gather | solution.py:128
  36.3 10.2 %all-gather.2 = bf16[8,8,64]{2,1,0:T(8,128)(2,1)S(1)} all-gather(bf16[2,8,64]{2,1,0:T(8,128)(2,1)S(1)} %pad_maximum_fusion), channel_id=4, replica_groups=mesh['src'=4,'tgt'=8] {'src'}, dimensions={0}, use_global_device_ids=true | all-gather | bytes 10240 | tf_op jit(solution)/shard_map/all_gather | solution.py:131
  48.7 10.4 %sweep.4 = (f32[8,256]{1,0:T(8,128)S(1)}, f32[8,256]{1,0:T(8,128)S(1)}) custom-call(s32[8,8]{1,0:T(8,128)S(1)} %copy-done, bf16[8,8,32,128]{3,2,1,0:T(8,128)(2,1)S(1)} %bitcast.26, bf16[4,8,64,128]{3,2,1,0:T(8,128)(2,1)S(1)} %bitcast.32, f32[8,256]{1,0:T(8,128)S(1)} %get-tuple-element.41.u_ref, f32[8,256]{1,0:T(8,128)S(1)} %get-tuple-element.39.h_ref), custom_call_target="tpu_custom_call" | custom-call | tf_op jit(solution)/shard_map/sweep/pallas_call | solution.py:174
  59.1 10.2 %all-gather.4 = f32[32,256]{1,0:T(8,128)S(1)} all-gather(f32[8,256]{1,0:T(8,128)S(1)} %get-tuple-element.13), channel_id=6, replica_groups=mesh['src'=4,'tgt'=8] {'src'}, dimensions={0}, use_global_device_ids=true | all-gather | bytes 40960 | tf_op jit(solution)/shard_map/all_gather | solution.py:114
  69.3 22.0 %all-gather.5 = f32[64,256]{1,0:T(8,128)S(1)} all-gather(f32[8,256]{1,0:T(8,128)S(1)} %get-tuple-element.14), channel_id=7, replica_groups=mesh['src'=4,'tgt'=8] {'tgt'}, dimensions={0}, use_global_device_ids=true | all-gather | bytes 73728 | tf_op jit(solution)/shard_map/all_gather | solution.py:114
  91.4 10.4 %sweep.5 = (f32[8,256]{1,0:T(8,128)S(1)}, f32[8,256]{1,0:T(8,128)S(1)}) custom-call(s32[8,8]{1,0:T(8,128)S(1)} %copy-done, bf16[8,8,32,128]{3,2,1,0:T(8,128)(2,1)S(1)} %bitcast.27, bf16[4,8,64,128]{3,2,1,0:T(8,128)(2,1)S(1)} %bitcast.33, f32[8,256]{1,0:T(8,128)S(1)} %get-tuple-element.37.u_ref, f32[8,256]{1,0:T(8,128)S(1)} %get-tuple-element.35.h_ref), custom_call_target="tpu_custom_call" | custom-call | tf_op jit(solution)/shard_map/sweep/pallas_call | solution.py:174
  101.9 12.4 %all-gather.7 = f32[64,256]{1,0:T(8,128)S(1)} all-gather(f32[8,256]{1,0:T(8,128)S(1)} %get-tuple-element.16), channel_id=9, replica_groups=mesh['src'=4,'tgt'=8] {'tgt'}, dimensions={0}, use_global_device_ids=true | all-gather | bytes 73728 | tf_op jit(solution)/shard_map/all_gather | solution.py:114
  114.3 10.2 %all-gather.6 = f32[32,256]{1,0:T(8,128)S(1)} all-gather(f32[8,256]{1,0:T(8,128)S(1)} %get-tuple-element.15), channel_id=8, replica_groups=mesh['src'=4,'tgt'=8] {'src'}, dimensions={0}, use_global_device_ids=true | all-gather | bytes 40960 | tf_op jit(solution)/shard_map/all_gather | solution.py:114
  124.6 10.4 %sweep.6 = (f32[8,256]{1,0:T(8,128)S(1)}, f32[8,256]{1,0:T(8,128)S(1)}) custom-call(s32[8,8]{1,0:T(8,128)S(1)} %copy-done, bf16[8,8,32,128]{3,2,1,0:T(8,128)(2,1)S(1)} %bitcast.28, bf16[4,8,64,128]{3,2,1,0:T(8,128)(2,1)S(1)} %bitcast.34, f32[8,256]{1,0:T(8,128)S(1)} %get-tuple-element.33.u_ref, f32[8,256]{1,0:T(8,128)S(1)} %get-tuple-element.31.h_ref), custom_call_target="tpu_custom_call" | custom-call | tf_op jit(solution)/shard_map/sweep/pallas_call | solution.py:174
  135.1 15.0 %all-gather.9 = f32[64,256]{1,0:T(8,128)S(1)} all-gather(f32[8,256]{1,0:T(8,128)S(1)} %get-tuple-element.18), channel_id=11, replica_groups=mesh['src'=4,'tgt'=8] {'tgt'}, dimensions={0}, use_global_device_ids=true | all-gather | bytes 73728 | tf_op jit(solution)/shard_map/all_gather | solution.py:114
  150.1 10.2 %all-gather.8 = f32[32,256]{1,0:T(8,128)S(1)} all-gather(f32[8,256]{1,0:T(8,128)S(1)} %get-tuple-element.17), channel_id=10, replica_groups=mesh['src'=4,'tgt'=8] {'src'}, dimensions={0}, use_global_device_ids=true | all-gather | bytes 40960 | tf_op jit(solution)/shard_map/all_gather | solution.py:114
  160.5 10.4 %sweep.7 = (f32[8,256]{1,0:T(8,128)S(1)}, f32[8,256]{1,0:T(8,128)S(1)}) custom-call(s32[8,8]{1,0:T(8,128)S(1)} %copy-done, bf16[8,8,32,128]{3,2,1,0:T(8,128)(2,1)S(1)} %bitcast.29, bf16[4,8,64,128]{3,2,1,0:T(8,128)(2,1)S(1)} %bitcast.35, f32[8,256]{1,0:T(8,128)S(1)} %get-tuple-element.29.u_ref, f32[8,256]{1,0:T(8,128)S(1)} %get-tuple-element.27.h_ref), custom_call_target="tpu_custom_call" | custom-call | tf_op jit(solution)/shard_map/sweep/pallas_call | solution.py:174
  170.9 10.5 %all-gather.10 = f32[32,256]{1,0:T(8,128)S(1)} all-gather(f32[8,256]{1,0:T(8,128)S(1)} %get-tuple-element.19), channel_id=12, replica_groups=mesh['src'=4,'tgt'=8] {'src'}, dimensions={0}, use_global_device_ids=true | all-gather | bytes 40960 | tf_op jit(solution)/shard_map/all_gather | solution.py:114
  181.5 11.4 %project.1 = (f32[8,256,128]{2,1,0:T(8,128)S(1)}, f32[8,256]{1,0:T(8,128)S(1)}) custom-call(s32[8,8]{1,0:T(8,128)S(1)} %copy-done, bf16[8,8,32,128]{3,2,1,0:T(8,128)(2,1)S(1)} %bitcast.30, bf16[4,8,64,128]{3,2,1,0:T(8,128)(2,1)S(1)} %bitcast.36, f32[8,256]{1,0:T(8,128)S(1)} %get-tuple-element.25.h_ref), custom_call_target="tpu_custom_call" | custom-call | tf_op jit(solution)/shard_map/project/pallas_call | solution.py:181
  192.9 23.4 %all-gather.11 = f32[64,256]{1,0:T(8,128)S(1)} all-gather(f32[8,256]{1,0:T(8,128)S(1)} %get-tuple-element.21), channel_id=13, replica_groups=mesh['src'=4,'tgt'=8] {'tgt'}, dimensions={0}, use_global_device_ids=true | all-gather | bytes 73728 | tf_op jit(solution)/shard_map/all_gather | solution.py:114
  216.7 1.1 copy.18
  217.8 3.6 %all-to-all-start = ((f32[1,8,8,32,128]{4,3,1,0,2:T(8,128)}), f32[1,8,8,32,128]{4,3,1,0,2:T(8,128)S(1)}, u32[]{:S(2)}, u32[]{:S(2)}) async-start(f32[1,8,8,32,128]{4,3,1,0,2:T(8,128)} %copy.18), calls=%async_computation | async-start | bytes 2097152 | tf_op jit(solution)/shard_map/all_to_all | solution.py:184
  221.4 18.7 %all-gather.12 = f32[64,256]{1,0:T(8,128)S(1)} all-gather(f32[8,256]{1,0:T(8,128)S(1)} %get-tuple-element.22), channel_id=14, replica_groups=mesh['src'=4,'tgt'=8] {'tgt'}, dimensions={0}, use_global_device_ids=true | all-gather | bytes 73728 | tf_op jit(solution)/shard_map/all_gather | solution.py:114
  240.1 0.7 dynamic-slice_multiply_fusion
  240.8 0.7 fusion.2
  241.5 0.7 reduce_sum.29
  (46 shorter events, 5.4 us)
Async XLA Ops:
  11.7 0.7 copy-start.5
  11.8 0.7 copy-start.4
  21.2 0.9 copy-start.1
  35.5 0.7 copy-start.7
  35.6 0.7 copy-start.6
  46.7 0.7 copy-start.3
  47.3 0.7 copy-start.2
  48.0 0.7 copy-start
  217.8 23.7 %all-to-all-start = ((f32[1,8,8,32,128]{4,3,1,0,2:T(8,128)}), f32[1,8,8,32,128]{4,3,1,0,2:T(8,128)S(1)}, u32[]{:S(2)}, u32[]{:S(2)}) async-start(f32[1,8,8,32,128]{4,3,1,0,2:T(8,128)} %copy.18), calls=%async_computation | async-start | bytes 2097152 | tf_op jit(solution)/shard_map/all_to_all | solution.py:184

commit v2 on v1

v2 whole, which is shorter than its diff:
```python
import functools
import math

import jax
import jax.numpy as jnp
from jax import lax
from jax.experimental import pallas as pl
from jax.experimental.pallas import tpu as pltpu
from jax.sharding import PartitionSpec as P

ITERS = 4
EPSILON = 0.1
UNIT = 1.0 / (EPSILON * math.log(2.0))
FLOOR = -1e30
LANES = 128
GROUP = 4

SMEM = pl.BlockSpec(memory_space=pltpu.SMEM)
VMEM = pl.BlockSpec(memory_space=pltpu.VMEM)
PARAMS = pltpu.CompilerParams(vmem_limit_bytes=40 * 1024 * 1024)


def f32(*shape):
    return jax.ShapeDtypeStruct(shape, jnp.float32)


def swap(part, axis, mask):
    return lax.ppermute(part, axis, [(i, i ^ mask) for i in range(lax.axis_size(axis))])


def near_count(axis):
    return lax.axis_size(axis) // 4


def merge_lse(parts):
    top = functools.reduce(jnp.maximum, parts)
    return top + jnp.log2(sum(jnp.exp2(part - top) for part in parts))


def exchange_lse(part, axis):
    near = near_count(axis)
    if near > 1:
        part = merge_lse([part] + [swap(part, axis, d) for d in range(1, near)])
    return [part] + [swap(part, axis, near * k) for k in range(1, 4)]


def gather_pieces(piece, axis):
    near = near_count(axis)
    four = jnp.stack([piece] + [swap(piece, axis, near * k) for k in range(1, 4)])
    return [four] + [swap(four, axis, d) for d in range(1, near)]


def whole_block(ref, k):
    piece = ref[:, k]
    return piece.reshape(piece.shape[0] * piece.shape[1], piece.shape[2])


def spread_columns(vec, col_ref):
    turned = vec.T
    for k in range(vec.shape[0]):
        col_ref[k] = jnp.broadcast_to(turned[:, k : k + 1], col_ref.shape[1:])


def pair_dots(lhs_ref, p, rhs_ref, q):
    return lax.dot_general(
        whole_block(lhs_ref, p),
        whole_block(rhs_ref, q),
        (((1,), (1,)), ((), ())),
        preferred_element_type=jnp.float32,
    )


def column_lse(dots, col):
    score = dots * UNIT + jnp.concatenate([col] * (dots.shape[1] // LANES), axis=1)
    peak = jnp.max(score, axis=0, keepdims=True)
    return peak, jnp.sum(jnp.exp2(score - peak), axis=0, keepdims=True)


def clear(peak_ref, sum_ref):
    peak_ref[...] = jnp.full(peak_ref.shape, FLOOR, jnp.float32)
    sum_ref[...] = jnp.zeros(sum_ref.shape, jnp.float32)


def merge_slots(peak_ref, sum_ref, count):
    shape = (count, peak_ref.shape[0] // count, peak_ref.shape[1])
    peak = peak_ref[...].reshape(shape)
    top = jnp.max(peak, axis=1, keepdims=True)
    total = jnp.sum(sum_ref[...].reshape(shape) * jnp.exp2(peak - top), axis=1)
    return top[:, 0] + jnp.log2(jnp.maximum(total, 1.0))


def visit_pairs(count_ref, list_ref, tb, work):
    @pl.loop(0, pl.cdiv(count_ref[0], GROUP))
    def _(step):
        codes = [list_ref[step * GROUP + k] for k in range(GROUP)]
        work([(code // tb, lax.rem(code, tb)) for code in codes])


def sweep(count_ref, list_ref, x_ref, y_ref, u, h, rows_ref, cols_ref, scratch):
    ucol_ref, hcol_ref, rpeak_ref, rsum_ref, cpeak_ref, csum_ref = scratch
    sb, tb = x_ref.shape[1], y_ref.shape[1]
    spread_columns(u, ucol_ref)
    spread_columns(h, hcol_ref)
    clear(rpeak_ref, rsum_ref)
    clear(cpeak_ref, csum_ref)

    def work(pairs):
        found = []
        for p, q in pairs:
            row = column_lse(pair_dots(y_ref, q, x_ref, p), hcol_ref[q])
            col = column_lse(pair_dots(x_ref, p, y_ref, q), ucol_ref[p])
            found.append((p, q, row, col))
        for p, q, row, col in found:
            rpeak_ref[pl.ds(p * tb + q, 1), :], rsum_ref[pl.ds(p * tb + q, 1), :] = row
            cpeak_ref[pl.ds(q * sb + p, 1), :], csum_ref[pl.ds(q * sb + p, 1), :] = col

    visit_pairs(count_ref, list_ref, tb, work)
    rows_ref[...] = merge_slots(rpeak_ref, rsum_ref, sb)
    cols_ref[...] = merge_slots(cpeak_ref, csum_ref, tb)


def sweep_scratch(sb, tb, blk):
    return [
        pltpu.VMEM((sb, blk, LANES), jnp.float32),
        pltpu.VMEM((tb, blk, LANES), jnp.float32),
        pltpu.VMEM((sb * tb, blk), jnp.float32),
        pltpu.VMEM((sb * tb, blk), jnp.float32),
        pltpu.VMEM((sb * tb, blk), jnp.float32),
        pltpu.VMEM((sb * tb, blk), jnp.float32),
    ]


def list_kernel(keep_ref, count_ref, list_ref):
    sb, tb = keep_ref.shape

    def add(code, state):
        n, last = state
        kept = keep_ref[code // tb, lax.rem(code, tb)] > 0
        list_ref[n] = code
        return n + kept.astype(jnp.int32), jnp.where(kept, code, last)

    n, last = lax.fori_loop(0, sb * tb, add, (jnp.int32(0), jnp.int32(0)))
    for k in range(GROUP):
        list_ref[n + k] = last
    count_ref[0] = n


def assemble(place, counts_ref, four_refs, points_ref, vec_ref):
    n, blocks, piece, width = points_ref.shape
    blk = n * piece
    vec_ref[...] = jnp.zeros(vec_ref.shape, jnp.float32)
    for d, four_ref in enumerate(four_refs):
        for k in range(4):
            owner = jnp.bitwise_xor(place, len(four_refs) * k + d)
            points_ref[owner] = four_ref[k, : blocks * piece].reshape(blocks, piece, width)
            tile = owner * piece // LANES
            for v in range(2):
                start = blocks * piece + v * blocks
                vec_ref[v, tile] += four_ref[k, start : start + blocks].astype(jnp.float32)
    mass = jnp.concatenate([vec_ref[0, t] for t in range(blk // LANES)], axis=1)
    potential = jnp.concatenate([vec_ref[1, t] for t in range(blk // LANES)], axis=1) * UNIT
    block_of = lax.broadcasted_iota(jnp.int32, (blocks, blk), 0)
    slot_of = lax.broadcasted_iota(jnp.int32, (blocks, blk), 1)
    half = jnp.zeros((blocks, blk), jnp.float32)
    count = jnp.zeros((blocks, blk), jnp.int32)
    ones = jnp.ones((blocks, width), jnp.bfloat16)
    for k in range(blocks):
        wide = whole_block(points_ref, k).astype(jnp.float32)
        square = wide * wide
        high = square.astype(jnp.bfloat16)
        low = (square - high.astype(jnp.float32)).astype(jnp.bfloat16)
        norm = sum(
            lax.dot_general(ones, part, (((1,), (1,)), ((), ())), preferred_element_type=jnp.float32)
            for part in (high, low)
        )
        half = jnp.where(block_of == k, norm * (0.5 * UNIT), half)
        count = jnp.where(block_of == k, counts_ref[k], count)
    base = jnp.where(slot_of < count, jnp.log2(mass) - half, FLOOR)
    return potential, half, base


def first_kernel(nx, ny, place_ref, src_counts_ref, tgt_counts_ref, count_ref, list_ref, *refs):
    x_fours, y_fours, refs = refs[:nx], refs[nx : nx + ny], refs[nx + ny :]
    x_ref, y_ref, fixed_ref, f_ref, g_ref, rows_ref, cols_ref, xvec_ref, yvec_ref = refs[:9]
    f, x_half, x_base = assemble(place_ref[1], src_counts_ref, x_fours, x_ref, xvec_ref)
    g, y_half, y_base = assemble(place_ref[0], tgt_counts_ref, y_fours, y_ref, yvec_ref)
    f_ref[...] = f
    g_ref[...] = g
    for k, vec in enumerate((x_half, x_base, y_half, y_base)):
        fixed_ref[k] = vec
    sweep(count_ref, list_ref, x_ref, y_ref, f + x_base, g + y_base, rows_ref, cols_ref, refs[9:])


def updated(old, half, part_refs):
    return 0.5 * (old + (half - merge_lse([ref[...] for ref in part_refs])))


def step_kernel(count_ref, list_ref, x_ref, y_ref, fixed_ref, f_in_ref, g_in_ref, *refs):
    row_refs, col_refs, refs = refs[:4], refs[4:8], refs[8:]
    f_ref, g_ref, rows_ref, cols_ref = refs[:4]
    f = updated(f_in_ref[...], fixed_ref[0], row_refs)
    g = updated(g_in_ref[...], fixed_ref[2], col_refs)
    f_ref[...] = f
    g_ref[...] = g
    sweep(count_ref, list_ref, x_ref, y_ref, f + fixed_ref[1], g + fixed_ref[3], rows_ref, cols_ref, refs[4:])


def project_kernel(near, place_ref, count_ref, list_ref, x_ref, y_ref, fixed_ref, g_in_ref, *refs):
    col_refs, g_ref, out_refs = refs[:4], refs[4], refs[5 : 5 + near]
    h_ref, col_ref, peak_ref, sum_ref, acc_ref = refs[5 + near :]
    n, sb, piece, width = x_ref.shape
    tb = y_ref.shape[1]
    blk = n * piece
    g = updated(g_in_ref[...], fixed_ref[2], col_refs)
    g_ref[...] = g
    h = g + fixed_ref[3]
    h_ref[...] = h
    spread_columns(h, col_ref)
    clear(peak_ref, sum_ref)

    def measure(pairs):
        found = [(p * tb + q, column_lse(pair_dots(y_ref, q, x_ref, p), col_ref[q])) for p, q in pairs]
        for slot, row in found:
            peak_ref[pl.ds(slot, 1), :], sum_ref[pl.ds(slot, 1), :] = row

    visit_pairs(count_ref, list_ref, tb, measure)
    lse = merge_slots(peak_ref, sum_ref, sb)
    spread_columns(lse, col_ref)
    acc_ref[...] = jnp.zeros(acc_ref.shape, jnp.float32)

    def move(pairs):
        moves = []
        for p, q in pairs:
            ys = whole_block(y_ref, q)
            col = jnp.concatenate([col_ref[p]] * (blk // LANES), axis=1)
            weights = jnp.exp2(pair_dots(x_ref, p, y_ref, q) * UNIT + (h_ref[pl.ds(q, 1), :] - col))
            high = weights.astype(jnp.bfloat16)
            low = (weights - high.astype(jnp.float32)).astype(jnp.bfloat16)
            full = jnp.concatenate([ys, jnp.ones(ys.shape, ys.dtype)], axis=1)
            moves.append(
                jnp.dot(high, full, preferred_element_type=jnp.float32)
                + jnp.dot(low, full, preferred_element_type=jnp.float32)
            )
        return moves

    def move_all(pairs):
        for (p, _), moved in zip(pairs, move(pairs)):
            acc_ref[p] += moved

    @pl.loop(0, count_ref[0])
    def _(k):
        code = list_ref[k]
        move_all([(code // tb, lax.rem(code, tb))])

    me = lax.rem(place_ref[1], near)
    for p in range(sb):
        total = acc_ref[p, :, width:]
        image = acc_ref[p, :, :width] / jnp.where(total > 0.0, total, 1.0)
        acc_ref[p, :, :width] = image
    for e, out_ref in enumerate(out_refs):
        for far in range(4):
            owner = far * near + jnp.bitwise_xor(me, e)
            for p in range(sb):
                out_ref[far, p * piece : (p + 1) * piece] = acc_ref[p, pl.ds(owner * piece, piece), :width]
            left = lse[:, :LANES]
            for t in range(1, blk // LANES):
                left = jnp.where(owner * piece // LANES == t, lse[:, t * LANES : (t + 1) * LANES], left)
            out_ref[far, sb * piece :] = left


def merge_images(parts, offset, sb, piece, turn_ref):
    whole = merge_lse([lse for _, lse in parts])
    weights = []
    for k, (_, lse) in enumerate(parts):
        turn_ref[k] = jnp.exp2(lse - whole).T
        weights.append(turn_ref[k, pl.ds(offset, piece), :])
    images = []
    for p in range(sb):
        images.append(
            sum(
                image[p * piece : (p + 1) * piece] * weight[:, p : p + 1]
                for (image, _), weight in zip(parts, weights)
            )
        )
    return images, whole


def near_kernel(near, sb, piece, place_ref, *refs):
    in_refs, out_refs, turn_ref = refs[:near], refs[near : near + 4], refs[near + 4]
    me = lax.rem(place_ref[1], near)
    mine = place_ref[1] // near
    rows = sb * piece
    for d, out_ref in enumerate(out_refs):
        far = jnp.bitwise_xor(mine, d)
        offset = lax.rem((far * near + me) * piece, LANES)
        parts = [(ref[far, :rows], ref[far, rows:]) for ref in in_refs]
        images, whole = merge_images(parts, pl.multiple_of(offset, piece), sb, piece, turn_ref)
        for p in range(sb):
            out_ref[p * piece : (p + 1) * piece] = images[p]
        out_ref[rows:] = whole


def far_kernel(sb, piece, place_ref, *refs):
    in_refs, out_ref, turn_ref = refs[:4], refs[4], refs[5]
    rows = sb * piece
    offset = lax.rem(place_ref[1] * piece, LANES)
    parts = [(ref[:rows], ref[rows:]) for ref in in_refs]
    images, _ = merge_images(parts, pl.multiple_of(offset, piece), sb, piece, turn_ref)
    for p in range(sb):
        out_ref[p] = images[p]


def packed(points, mass, potential, axis):
    blocks, piece, width = points.shape
    here = lax.axis_index(axis) * piece % LANES
    lane = jnp.arange(LANES, dtype=jnp.int32)[None, :]
    inside = (lane >= here) & (lane < here + piece)

    def placed(vec):
        return jnp.where(inside, jnp.tile(vec, (1, LANES // piece)), 0)

    return jnp.concatenate([points.reshape(blocks * piece, width), placed(mass), placed(potential)])


def on_device(
    src_points, tgt_points, src_mass, tgt_mass, src_potential, tgt_potential, src_counts, tgt_counts, keep
):
    ntgt, nsrc = lax.axis_size("tgt"), lax.axis_size("src")
    near = near_count("tgt")
    sb, src_piece, width = src_points.shape
    tb, tgt_piece, _ = tgt_points.shape
    blk = src_piece * ntgt
    place = jnp.stack([lax.axis_index("src"), lax.axis_index("tgt")]).astype(jnp.int32)

    count, pairs = pl.pallas_call(
        list_kernel,
        out_shape=(
            jax.ShapeDtypeStruct((1,), jnp.int32),
            jax.ShapeDtypeStruct((sb * tb + GROUP,), jnp.int32),
        ),
        in_specs=[SMEM],
        out_specs=(SMEM, SMEM),
        name="kept_pairs",
    )(keep)

    y_fours = gather_pieces(packed(tgt_points, tgt_mass, tgt_potential, "src"), "src")
    x_fours = gather_pieces(packed(src_points, src_mass, src_potential, "tgt"), "tgt")

    vectors = (f32(sb, blk), f32(tb, blk), f32(sb, blk), f32(tb, blk))
    x, y, fixed, f, g, rows, cols = pl.pallas_call(
        functools.partial(first_kernel, len(x_fours), len(y_fours)),
        out_shape=(
            jax.ShapeDtypeStruct((ntgt, sb, src_piece, width), jnp.bfloat16),
            jax.ShapeDtypeStruct((nsrc, tb, tgt_piece, width), jnp.bfloat16),
            f32(4, sb, blk),
        )
        + vectors,
        in_specs=[SMEM] * 5 + [VMEM] * (len(x_fours) + len(y_fours)),
        out_specs=(VMEM,) * 7,
        scratch_shapes=[
            pltpu.VMEM((2, blk // LANES, sb, LANES), jnp.float32),
            pltpu.VMEM((2, blk // LANES, tb, LANES), jnp.float32),
        ]
        + sweep_scratch(sb, tb, blk),
        compiler_params=PARAMS,
        name="first_sweep",
    )(place, src_counts, tgt_counts, count, pairs, *x_fours, *y_fours)

    step = pl.pallas_call(
        step_kernel,
        out_shape=vectors,
        in_specs=[SMEM] * 2 + [VMEM] * 13,
        out_specs=(VMEM,) * 4,
        scratch_shapes=sweep_scratch(sb, tb, blk),
        compiler_params=PARAMS,
        name="sweep",
    )
    for _ in range(ITERS - 1):
        row_parts = exchange_lse(rows, "tgt")
        col_parts = exchange_lse(cols, "src")
        f, g, rows, cols = step(count, pairs, x, y, fixed, f, g, *row_parts, *col_parts)

    col_parts = exchange_lse(cols, "src")
    row_parts = exchange_lse(rows, "tgt")
    tile = sb * src_piece + sb
    g, *near_parts = pl.pallas_call(
        functools.partial(project_kernel, near),
        out_shape=(f32(tb, blk),) + (f32(4, tile, width),) * near,
        in_specs=[SMEM] * 3 + [VMEM] * 8,
        out_specs=(VMEM,) * (1 + near),
        scratch_shapes=[
            pltpu.VMEM((tb, blk), jnp.float32),
            pltpu.VMEM((max(sb, tb), blk, LANES), jnp.float32),
            pltpu.VMEM((sb * tb, blk), jnp.float32),
            pltpu.VMEM((sb * tb, blk), jnp.float32),
            pltpu.VMEM((sb, blk, 2 * width), jnp.float32),
        ],
        compiler_params=PARAMS,
        name="project",
    )(place, count, pairs, x, y, fixed, g, *col_parts)
    if near > 1:
        near_parts = near_parts[:1] + [swap(near_parts[d], "tgt", d) for d in range(1, near)]
    far_parts = pl.pallas_call(
        functools.partial(near_kernel, near, sb, src_piece),
        out_shape=(f32(tile, width),) * 4,
        in_specs=[SMEM] + [VMEM] * near,
        out_specs=(VMEM,) * 4,
        scratch_shapes=[pltpu.VMEM((near, LANES, sb), jnp.float32)],
        compiler_params=PARAMS,
        name="merge_near",
    )(place, *near_parts)
    far_parts = [far_parts[0]] + [swap(far_parts[k], "tgt", near * k) for k in range(1, 4)]
    images = pl.pallas_call(
        functools.partial(far_kernel, sb, src_piece),
        out_shape=f32(sb, src_piece, width),
        in_specs=[SMEM] + [VMEM] * 4,
        out_specs=VMEM,
        scratch_shapes=[pltpu.VMEM((4, LANES, sb), jnp.float32)],
        compiler_params=PARAMS,
        name="merge_far",
    )(place, *far_parts)

    f = 0.5 * (f + (fixed[0] - merge_lse(row_parts)))
    src_final = lax.dynamic_slice_in_dim(f * (1.0 / UNIT), place[1] * src_piece, src_piece, 1)
    tgt_final = lax.dynamic_slice_in_dim(g * (1.0 / UNIT), place[0] * tgt_piece, tgt_piece, 1)
    return images, src_final, tgt_final


def solution(mesh):
    return jax.shard_map(
        on_device,
        mesh=mesh,
        in_specs=(
            P("src", "tgt", None),
            P("tgt", "src", None),
            P("src", "tgt"),
            P("tgt", "src"),
            P("src", "tgt"),
            P("tgt", "src"),
            P("src"),
            P("tgt"),
            P("src", "tgt"),
        ),
        out_specs=(P("src", "tgt", None), P("src", "tgt"), P("tgt", "src")),
        check_vma=False,
    )
```

time: 244 us -> 118 us (0.48)
  the two profiles are of different devices: /device:TPU:25 before, /device:TPU:0 now
where the time goes in v2:
time: 118 us; the launch traced here: 119 us
  Pallas kernels  45.6 us (39%)
  starting transfers between devices  44.9 us (38%)
  waiting for transfers between devices  21.5 us (18%)
  local copies, waits for them, and re-layouts  4.45 us (4%)
  other arithmetic  1.68 us (1%)
    ppermute x39, starting transfers between devices, swap(): lax.ppermute(part, axis, [(i, i ^ mask) for i in range(lax.axis_size(axis...  44.9 us
    ppermute x39, waiting for transfers between devices, swap(): lax.ppermute(part, axis, [(i, i ^ mask) for i in range(lax.axis_size(axis...  21.5 us
    pallas_call x3, Pallas kernels, on_device(): step(count, pairs, x, y, fixed, f, g, *row_parts, *col_parts)  19.1 us
    pallas_call x1, Pallas kernels, on_device(): pl.pallas_call(functools.partial(project_kernel, near), out_shape=(f32(tb...  14.2 us
    pallas_call x1, Pallas kernels, on_device(): pl.pallas_call(functools.partial(first_kernel, len(x_fours), len(y_fours)...  7.06 us
    unnamed x14, local copies, waits for them, and re-layouts  2.72 us
    pallas_call x1, Pallas kernels, on_device(): pl.pallas_call(list_kernel, out_shape=(jax.ShapeDtypeStruct((1,), jnp.int...  2.46 us
  transfers between devices with their start and end apart: 39, of which 13 were waited for; matrix products, arithmetic and copies ran while one was open for 2% of the time, Pallas kernels for 15%

profile of v2, /device:TPU:0, one launch (start us, length us, event | category | flops | bytes accessed | tf_op | source)
XLA Modules:
  0.0 119.1 jit_solution(16071667626331290552)
XLA Ops:
  2.3 3.0 %collective-permute-start.1 = (bf16[272,128]{1,0:T(8,128)(2,1)S(1)}, bf16[272,128]{1,0:T(8,128)(2,1)S(1)}, u32[]{:S(2)}, u32[]{:S(2)}) collective-permute-start(bf16[272,128]{1,0:T(8,128)(2,1)S(1)} %get-tuple-element.62), channel_id=1, source_target_pairs={{0,4},{1,5},{2,6},{3,7},{4,0},{5,1},{6,2},{7,3},{8,12},{9,13},{10,... | collective-permute-start | bytes 208904 | tf_op jit(solution)/shard_map/ppermute | solution.py:28
  8.3 1.8 %collective-permute-done = bf16[272,128]{1,0:T(8,128)(2,1)S(1)} collective-permute-done((bf16[272,128]{1,0:T(8,128)(2,1)S(1)}, bf16[272,128]{1,0:T(8,128)(2,1)S(1)}, u32[]{:S(2)}, u32[]{:S(2)}) %collective-permute-start) | collective-permute-done | bytes 69664 | tf_op jit(solution)/shard_map/ppermute | solution.py:28
  10.1 1.9 %collective-permute-done.2 = bf16[272,128]{1,0:T(8,128)(2,1)S(1)} collective-permute-done((bf16[272,128]{1,0:T(8,128)(2,1)S(1)}, bf16[272,128]{1,0:T(8,128)(2,1)S(1)}, u32[]{:S(2)}, u32[]{:S(2)}) %collective-permute-start.2) | collective-permute-done | bytes 69664 | tf_op jit(solution)/shard_map/ppermute | solution.py:28
  12.9 2.7 %collective-permute-start.5 = (bf16[528,128]{1,0:T(8,128)(2,1)S(1)}, bf16[528,128]{1,0:T(8,128)(2,1)S(1)}, u32[]{:S(2)}, u32[]{:S(2)}) collective-permute-start(bf16[528,128]{1,0:T(8,128)(2,1)S(1)} %get-tuple-element.60), channel_id=1, source_target_pairs={{0,16},{8,24},{16,0},{24,8},{1,17},{9,25},{17,1},{25,9},{2,18},{10... | collective-permute-start | bytes 405512 | tf_op jit(solution)/shard_map/ppermute | solution.py:28
  17.4 2.5 %kept_pairs.1 = (s32[1]{0:T(128)}, s32[68]{0:T(128)}) custom-call(s32[8,8]{1,0:T(8,128)} %keep_ref.1), custom_call_target="tpu_custom_call" | custom-call | tf_op jit(solution)/shard_map/kept_pairs/pallas_call | solution.py:335
  19.9 6.1 %collective-permute-done.5 = bf16[528,128]{1,0:T(8,128)(2,1)S(1)} collective-permute-done((bf16[528,128]{1,0:T(8,128)(2,1)S(1)}, bf16[528,128]{1,0:T(8,128)(2,1)S(1)}, u32[]{:S(2)}, u32[]{:S(2)}) %collective-permute-start.5) | collective-permute-done | bytes 135200 | tf_op jit(solution)/shard_map/ppermute | solution.py:28
  26.8 7.1 %first_sweep.1 = (bf16[8,8,32,128]{3,2,1,0:T(8,128)(2,1)S(1)}, bf16[4,8,64,128]{3,2,1,0:T(8,128)(2,1)S(1)}, f32[4,8,256]{2,1,0:T(8,128)S(1)}, f32[8,256]{1,0:T(8...) custom-call(s32[2]{0:T(128)S(1)} %pad_add_fusion.place_ref, s32[8]{0:T(128)S(1)} %copy-done.1, ...), custom_call_target="tpu_custom_call" | custom-call | tf_op jit(solution)/shard_map/first_sweep/pallas_call | solution.py:350
  34.0 3.8 %collective-permute-start.12 = (f32[8,256]{1,0:T(8,128)S(1)}, f32[8,256]{1,0:T(8,128)S(1)}, u32[]{:S(2)}, u32[]{:S(2)}) collective-permute-start(f32[8,256]{1,0:T(8,128)S(1)} %get-tuple-element.39.refs_4_), channel_id=1, source_target_pairs={{0,16},{8,24},{16,0},{24,8},{1,17},{9,25},{17,1},{25,9},{2,18},{10... | collective-permute-start | bytes 24584 | tf_op jit(solution)/shard_map/ppermute | solution.py:28
  38.5 2.2 %collective-permute-start.9 = (f32[8,256]{1,0:T(8,128)S(1)}, f32[8,256]{1,0:T(8,128)S(1)}, u32[]{:S(2)}, u32[]{:S(2)}) collective-permute-start(f32[8,256]{1,0:T(8,128)S(1)} %multiply_add_fusion.3.refs_0_), channel_id=1, source_target_pairs={{0,4},{1,5},{2,6},{3,7},{4,0},{5,1},{6,2},{7,3},{8,12},{9,13},{10,... | collective-permute-start | bytes 24584 | tf_op jit(solution)/shard_map/ppermute | solution.py:28
  44.3 6.4 %sweep.3 = (f32[8,256]{1,0:T(8,128)S(1)}, f32[8,256]{1,0:T(8,128)S(1)}, f32[8,256]{1,0:T(8,128)S(1)}, f32[8,256]{1,0:T(8,128)S(1)}) custom-call(s32[1]{0:T(128)} %get-tuple-element.31.count_ref, s32[68]{0:T(128)S(1)} %copy-done, bf16[8,8,32,128]{3,2,1,0:T(8,128)(2,1)S(1)} %get-tuple-element.33.x_ref, bf16[4,8,64,128]{3,2,1,0:T(8,128)(2,1)S(1)} %get-tuple-element.34.y_ref, ...), custom_call_target="tpu_custom_call" | custom-call | tf_op jit(solution)/shard_map/sweep/pallas_call | solution.py:381
  50.9 1.6 %collective-permute-start.19 = (f32[8,256]{1,0:T(8,128)S(1)}, f32[8,256]{1,0:T(8,128)S(1)}, u32[]{:S(2)}, u32[]{:S(2)}) collective-permute-start(f32[8,256]{1,0:T(8,128)S(1)} %get-tuple-element.43.refs_4_), channel_id=1, source_target_pairs={{0,16},{8,24},{16,0},{24,8},{1,17},{9,25},{17,1},{25,9},{2,18},{10... | collective-permute-start | bytes 24584 | tf_op jit(solution)/shard_map/ppermute | solution.py:28
  52.5 2.8 %collective-permute-start.18 = (f32[8,256]{1,0:T(8,128)S(1)}, f32[8,256]{1,0:T(8,128)S(1)}, u32[]{:S(2)}, u32[]{:S(2)}) collective-permute-start(f32[8,256]{1,0:T(8,128)S(1)} %get-tuple-element.43.refs_4_), channel_id=1, source_target_pairs={{0,8},{8,0},{16,24},{24,16},{1,9},{9,1},{17,25},{25,17},{2,10},{10... | collective-permute-start | bytes 24584 | tf_op jit(solution)/shard_map/ppermute | solution.py:28
  55.3 2.0 %collective-permute-start.16 = (f32[8,256]{1,0:T(8,128)S(1)}, f32[8,256]{1,0:T(8,128)S(1)}, u32[]{:S(2)}, u32[]{:S(2)}) collective-permute-start(f32[8,256]{1,0:T(8,128)S(1)} %multiply_add_fusion.2.refs_0_), channel_id=1, source_target_pairs={{0,4},{1,5},{2,6},{3,7},{4,0},{5,1},{6,2},{7,3},{8,12},{9,13},{10,... | collective-permute-start | bytes 24584 | tf_op jit(solution)/shard_map/ppermute | solution.py:28
  61.0 6.4 %sweep.4 = (f32[8,256]{1,0:T(8,128)S(1)}, f32[8,256]{1,0:T(8,128)S(1)}, f32[8,256]{1,0:T(8,128)S(1)}, f32[8,256]{1,0:T(8,128)S(1)}) custom-call(s32[1]{0:T(128)} %get-tuple-element.31.count_ref, s32[68]{0:T(128)S(1)} %copy-done, bf16[8,8,32,128]{3,2,1,0:T(8,128)(2,1)S(1)} %get-tuple-element.33.x_ref, bf16[4,8,64,128]{3,2,1,0:T(8,128)(2,1)S(1)} %get-tuple-element.34.y_ref, ...), custom_call_target="tpu_custom_call" | custom-call | tf_op jit(solution)/shard_map/sweep/pallas_call | solution.py:381
  69.0 2.9 %collective-permute-start.25 = (f32[8,256]{1,0:T(8,128)S(1)}, f32[8,256]{1,0:T(8,128)S(1)}, u32[]{:S(2)}, u32[]{:S(2)}) collective-permute-start(f32[8,256]{1,0:T(8,128)S(1)} %get-tuple-element.47.refs_4_), channel_id=1, source_target_pairs={{0,8},{8,0},{16,24},{24,16},{1,9},{9,1},{17,25},{25,17},{2,10},{10... | collective-permute-start | bytes 24584 | tf_op jit(solution)/shard_map/ppermute | solution.py:28
  73.2 2.2 %collective-permute-start.22 = (f32[8,256]{1,0:T(8,128)S(1)}, f32[8,256]{1,0:T(8,128)S(1)}, u32[]{:S(2)}, u32[]{:S(2)}) collective-permute-start(f32[8,256]{1,0:T(8,128)S(1)} %multiply_add_fusion.1.refs_0_), channel_id=1, source_target_pairs={{0,2},{1,3},{2,0},{3,1},{4,6},{5,7},{6,4},{7,5},{8,10},{9,11},{10,... | collective-permute-start | bytes 24584 | tf_op jit(solution)/shard_map/ppermute | solution.py:28
  77.1 6.4 %sweep.5 = (f32[8,256]{1,0:T(8,128)S(1)}, f32[8,256]{1,0:T(8,128)S(1)}, f32[8,256]{1,0:T(8,128)S(1)}, f32[8,256]{1,0:T(8,128)S(1)}) custom-call(s32[1]{0:T(128)} %get-tuple-element.31.count_ref, s32[68]{0:T(128)S(1)} %copy-done, bf16[8,8,32,128]{3,2,1,0:T(8,128)(2,1)S(1)} %get-tuple-element.33.x_ref, bf16[4,8,64,128]{3,2,1,0:T(8,128)(2,1)S(1)} %get-tuple-element.34.y_ref, ...), custom_call_target="tpu_custom_call" | custom-call | tf_op jit(solution)/shard_map/sweep/pallas_call | solution.py:381
  84.7 3.2 %collective-permute-start.28 = (f32[8,256]{1,0:T(8,128)S(1)}, f32[8,256]{1,0:T(8,128)S(1)}, u32[]{:S(2)}, u32[]{:S(2)}) collective-permute-start(f32[8,256]{1,0:T(8,128)S(1)} %get-tuple-element.49.refs_0_), channel_id=1, source_target_pairs={{0,8},{8,0},{16,24},{24,16},{1,9},{9,1},{17,25},{25,17},{2,10},{10... | collective-permute-start | bytes 24584 | tf_op jit(solution)/shard_map/ppermute | solution.py:28
  89.5 14.2 %project.1 = (f32[8,256]{1,0:T(8,128)S(1)}, f32[4,264,128]{2,1,0:T(8,128)S(1)}, f32[4,264,128]{2,1,0:T(8,128)S(1)}) custom-call(s32[2]{0:T(128)S(1)} %pad_add_fusion.place_ref, s32[1]{0:T(128)} %get-tuple-element.31.count_ref, s32[68]{0:T(128)S(1)} %copy-done, bf16[8,8,32,128]{3,2,1,0:T(8,128)(2,1)S(1)} %get-tuple-element.33.x_ref, ...), custom_call_target="tpu_custom_call" | custom-call | tf_op jit(solution)/shard_map/project/pallas_call | solution.py:386
  104.0 3.4 %collective-permute-start.36 = (f32[8,256]{1,0:T(8,128)S(1)}, f32[8,256]{1,0:T(8,128)S(1)}, u32[]{:S(2)}, u32[]{:S(2)}) collective-permute-start(f32[8,256]{1,0:T(8,128)S(1)} %multiply_add_fusion), channel_id=1, source_target_pairs={{0,2},{1,3},{2,0},{3,1},{4,6},{5,7},{6,4},{7,5},{8,10},{9,11},{10,... | collective-permute-start | bytes 24584 | tf_op jit(solution)/shard_map/ppermute | solution.py:28
  110.0 2.8 %collective-permute-start.34 = (f32[264,128]{1,0:T(8,128)S(1)}, f32[264,128]{1,0:T(8,128)S(1)}, u32[]{:S(2)}, u32[]{:S(2)}) collective-permute-start(f32[264,128]{1,0:T(8,128)S(1)} %get-tuple-element.55), channel_id=1, source_target_pairs={{0,6},{1,7},{2,4},{3,5},{4,2},{5,3},{6,0},{7,1},{8,14},{9,15},{10,... | collective-permute-start | bytes 405512 | tf_op jit(solution)/shard_map/ppermute | solution.py:28
  113.6 2.3 %collective-permute-done.32.refs_1_ = f32[264,128]{1,0:T(8,128)S(1)} collective-permute-done((f32[264,128]{1,0:T(8,128)S(1)}, f32[264,128]{1,0:T(8,128)S(1)}, u32[]{:S(2)}, u32[]{:S(2)}) %collective-permute-start.32) | collective-permute-done | bytes 135200 | tf_op jit(solution)/shard_map/ppermute | solution.py:28
  115.9 1.6 %collective-permute-done.33.refs_2_ = f32[264,128]{1,0:T(8,128)S(1)} collective-permute-done((f32[264,128]{1,0:T(8,128)S(1)}, f32[264,128]{1,0:T(8,128)S(1)}, u32[]{:S(2)}, u32[]{:S(2)}) %collective-permute-start.33) | collective-permute-done | bytes 135200 | tf_op jit(solution)/shard_map/ppermute | solution.py:28
  117.5 1.6 %merge_far.1 = f32[8,32,128]{2,1,0:T(8,128)} custom-call(s32[2]{0:T(128)S(1)} %pad_add_fusion.place_ref, f32[264,128]{1,0:T(8,128)S(1)} %get-tuple-element.52.refs_0_, f32[264,128]{1,0:T(8,128)S(1)} %collective-permute-done.32.refs_1_, f32[264,128]{1,0:T(8,128)S(1)} %collective-permute-done.33.refs_2_, f32[264,128]{1,0:T(8,128)S(1)} %collective-permute-done.34.refs_3_), custom_call_target="tpu_custom_call" | custom-call | tf_op jit(solution)/shard_map/merge_far/pallas_call | solution.py:413
  (101 shorter events, 27.4 us)
Async XLA Ops:
  2.3 6.0 %collective-permute-start.1 = (bf16[272,128]{1,0:T(8,128)(2,1)S(1)}, bf16[272,128]{1,0:T(8,128)(2,1)S(1)}, u32[]{:S(2)}, u32[]{:S(2)}) collective-permute-start(bf16[272,128]{1,0:T(8,128)(2,1)S(1)} %get-tuple-element.62), channel_id=1, source_target_pairs={{0,4},{1,5},{2,6},{3,7},{4,0},{5,1},{6,2},{7,3},{8,12},{9,13},{10,... | collective-permute-start | bytes 208904 | tf_op jit(solution)/shard_map/ppermute | solution.py:28
  6.8 5.2 %collective-permute-start.2 = (bf16[272,128]{1,0:T(8,128)(2,1)S(1)}, bf16[272,128]{1,0:T(8,128)(2,1)S(1)}, u32[]{:S(2)}, u32[]{:S(2)}) collective-permute-start(bf16[272,128]{1,0:T(8,128)(2,1)S(1)} %get-tuple-element.62), channel_id=1, source_target_pairs={{0,6},{1,7},{2,4},{3,5},{4,2},{5,3},{6,0},{7,1},{8,14},{9,15},{10,... | collective-permute-start | bytes 208904 | tf_op jit(solution)/shard_map/ppermute | solution.py:28
  12.0 14.1 %collective-permute-start.3 = (bf16[4,272,128]{2,1,0:T(8,128)(2,1)S(1)}, bf16[4,272,128]{2,1,0:T(8,128)(2,1)S(1)}, u32[]{:S(2)}, u32[]{:S(2)}) collective-permute-start(bf16[4,272,128]{2,1,0:T(8,128)(2,1)S(1)} %pad_maximum_fusion.1.refs_0_), channel_id=1, source_target_pairs={{0,1},{1,0},{2,3},{3,2},{4,5},{5,4},{6,7},{7,6},{8,9},{9,8},{10,11... | collective-permute-start | bytes 835592 | tf_op jit(solution)/shard_map/ppermute | solution.py:28
  12.9 13.1 %collective-permute-start.5 = (bf16[528,128]{1,0:T(8,128)(2,1)S(1)}, bf16[528,128]{1,0:T(8,128)(2,1)S(1)}, u32[]{:S(2)}, u32[]{:S(2)}) collective-permute-start(bf16[528,128]{1,0:T(8,128)(2,1)S(1)} %get-tuple-element.60), channel_id=1, source_target_pairs={{0,16},{8,24},{16,0},{24,8},{1,17},{9,25},{17,1},{25,9},{2,18},{10... | collective-permute-start | bytes 405512 | tf_op jit(solution)/shard_map/ppermute | solution.py:28
  15.6 10.5 %collective-permute-start.4 = (bf16[528,128]{1,0:T(8,128)(2,1)S(1)}, bf16[528,128]{1,0:T(8,128)(2,1)S(1)}, u32[]{:S(2)}, u32[]{:S(2)}) collective-permute-start(bf16[528,128]{1,0:T(8,128)(2,1)S(1)} %get-tuple-element.60), channel_id=1, source_target_pairs={{0,8},{8,0},{16,24},{24,16},{1,9},{9,1},{17,25},{25,17},{2,10},{10... | collective-permute-start | bytes 405512 | tf_op jit(solution)/shard_map/ppermute | solution.py:28
  17.1 8.9 %collective-permute-start.6 = (bf16[528,128]{1,0:T(8,128)(2,1)S(1)}, bf16[528,128]{1,0:T(8,128)(2,1)S(1)}, u32[]{:S(2)}, u32[]{:S(2)}) collective-permute-start(bf16[528,128]{1,0:T(8,128)(2,1)S(1)} %get-tuple-element.60), channel_id=1, source_target_pairs={{0,24},{8,16},{16,8},{24,0},{1,25},{9,17},{17,9},{25,1},{2,26},{10... | collective-permute-start | bytes 405512 | tf_op jit(solution)/shard_map/ppermute | solution.py:28
  33.9 6.7 %collective-permute-start.13 = (f32[8,256]{1,0:T(8,128)S(1)}, f32[8,256]{1,0:T(8,128)S(1)}, u32[]{:S(2)}, u32[]{:S(2)}) collective-permute-start(f32[8,256]{1,0:T(8,128)S(1)} %get-tuple-element.39.refs_4_), channel_id=1, source_target_pairs={{0,24},{8,16},{16,8},{24,0},{1,25},{9,17},{17,9},{25,1},{2,26},{10... | collective-permute-start | bytes 24584 | tf_op jit(solution)/shard_map/ppermute | solution.py:28
  34.0 8.0 %collective-permute-start.12 = (f32[8,256]{1,0:T(8,128)S(1)}, f32[8,256]{1,0:T(8,128)S(1)}, u32[]{:S(2)}, u32[]{:S(2)}) collective-permute-start(f32[8,256]{1,0:T(8,128)S(1)} %get-tuple-element.39.refs_4_), channel_id=1, source_target_pairs={{0,16},{8,24},{16,0},{24,8},{1,17},{9,25},{17,1},{25,9},{2,18},{10... | collective-permute-start | bytes 24584 | tf_op jit(solution)/shard_map/ppermute | solution.py:28
  50.8 6.5 %collective-permute-start.20 = (f32[8,256]{1,0:T(8,128)S(1)}, f32[8,256]{1,0:T(8,128)S(1)}, u32[]{:S(2)}, u32[]{:S(2)}) collective-permute-start(f32[8,256]{1,0:T(8,128)S(1)} %get-tuple-element.43.refs_4_), channel_id=1, source_target_pairs={{0,24},{8,16},{16,8},{24,0},{1,25},{9,17},{17,9},{25,1},{2,26},{10... | collective-permute-start | bytes 24584 | tf_op jit(solution)/shard_map/ppermute | solution.py:28
  50.9 8.0 %collective-permute-start.19 = (f32[8,256]{1,0:T(8,128)S(1)}, f32[8,256]{1,0:T(8,128)S(1)}, u32[]{:S(2)}, u32[]{:S(2)}) collective-permute-start(f32[8,256]{1,0:T(8,128)S(1)} %get-tuple-element.43.refs_4_), channel_id=1, source_target_pairs={{0,16},{8,24},{16,0},{24,8},{1,17},{9,25},{17,1},{25,9},{2,18},{10... | collective-permute-start | bytes 24584 | tf_op jit(solution)/shard_map/ppermute | solution.py:28
  52.5 6.4 %collective-permute-start.18 = (f32[8,256]{1,0:T(8,128)S(1)}, f32[8,256]{1,0:T(8,128)S(1)}, u32[]{:S(2)}, u32[]{:S(2)}) collective-permute-start(f32[8,256]{1,0:T(8,128)S(1)} %get-tuple-element.43.refs_4_), channel_id=1, source_target_pairs={{0,8},{8,0},{16,24},{24,16},{1,9},{9,1},{17,25},{25,17},{2,10},{10... | collective-permute-start | bytes 24584 | tf_op jit(solution)/shard_map/ppermute | solution.py:28
  67.4 5.8 %collective-permute-start.27 = (f32[8,256]{1,0:T(8,128)S(1)}, f32[8,256]{1,0:T(8,128)S(1)}, u32[]{:S(2)}, u32[]{:S(2)}) collective-permute-start(f32[8,256]{1,0:T(8,128)S(1)} %get-tuple-element.47.refs_4_), channel_id=1, source_target_pairs={{0,24},{8,16},{16,8},{24,0},{1,25},{9,17},{17,9},{25,1},{2,26},{10... | collective-permute-start | bytes 24584 | tf_op jit(solution)/shard_map/ppermute | solution.py:28
  67.5 8.0 %collective-permute-start.26 = (f32[8,256]{1,0:T(8,128)S(1)}, f32[8,256]{1,0:T(8,128)S(1)}, u32[]{:S(2)}, u32[]{:S(2)}) collective-permute-start(f32[8,256]{1,0:T(8,128)S(1)} %get-tuple-element.47.refs_4_), channel_id=1, source_target_pairs={{0,16},{8,24},{16,0},{24,8},{1,17},{9,25},{17,1},{25,9},{2,18},{10... | collective-permute-start | bytes 24584 | tf_op jit(solution)/shard_map/ppermute | solution.py:28
  69.0 6.5 %collective-permute-start.25 = (f32[8,256]{1,0:T(8,128)S(1)}, f32[8,256]{1,0:T(8,128)S(1)}, u32[]{:S(2)}, u32[]{:S(2)}) collective-permute-start(f32[8,256]{1,0:T(8,128)S(1)} %get-tuple-element.47.refs_4_), channel_id=1, source_target_pairs={{0,8},{8,0},{16,24},{24,16},{1,9},{9,1},{17,25},{25,17},{2,10},{10... | collective-permute-start | bytes 24584 | tf_op jit(solution)/shard_map/ppermute | solution.py:28
  83.4 5.5 %collective-permute-start.30 = (f32[8,256]{1,0:T(8,128)S(1)}, f32[8,256]{1,0:T(8,128)S(1)}, u32[]{:S(2)}, u32[]{:S(2)}) collective-permute-start(f32[8,256]{1,0:T(8,128)S(1)} %get-tuple-element.49.refs_0_), channel_id=1, source_target_pairs={{0,24},{8,16},{16,8},{24,0},{1,25},{9,17},{17,9},{25,1},{2,26},{10... | collective-permute-start | bytes 24584 | tf_op jit(solution)/shard_map/ppermute | solution.py:28
  83.5 5.4 %collective-permute-start.29 = (f32[8,256]{1,0:T(8,128)S(1)}, f32[8,256]{1,0:T(8,128)S(1)}, u32[]{:S(2)}, u32[]{:S(2)}) collective-permute-start(f32[8,256]{1,0:T(8,128)S(1)} %get-tuple-element.49.refs_0_), channel_id=1, source_target_pairs={{0,16},{8,24},{16,0},{24,8},{1,17},{9,25},{17,1},{25,9},{2,18},{10... | collective-permute-start | bytes 24584 | tf_op jit(solution)/shard_map/ppermute | solution.py:28
  84.7 4.8 %collective-permute-start.28 = (f32[8,256]{1,0:T(8,128)S(1)}, f32[8,256]{1,0:T(8,128)S(1)}, u32[]{:S(2)}, u32[]{:S(2)}) collective-permute-start(f32[8,256]{1,0:T(8,128)S(1)} %get-tuple-element.49.refs_0_), channel_id=1, source_target_pairs={{0,8},{8,0},{16,24},{24,16},{1,9},{9,1},{17,25},{25,17},{2,10},{10... | collective-permute-start | bytes 24584 | tf_op jit(solution)/shard_map/ppermute | solution.py:28
  87.9 16.0 %collective-permute-start.35 = (f32[8,256]{1,0:T(8,128)S(1)}, f32[8,256]{1,0:T(8,128)S(1)}, u32[]{:S(2)}, u32[]{:S(2)}) collective-permute-start(f32[8,256]{1,0:T(8,128)S(1)} %get-tuple-element.57), channel_id=1, source_target_pairs={{0,1},{1,0},{2,3},{3,2},{4,5},{5,4},{6,7},{7,6},{8,9},{9,8},{10,11... | collective-permute-start | bytes 24584 | tf_op jit(solution)/shard_map/ppermute | solution.py:28
  103.9 6.1 %collective-permute-start.38 = (f32[8,256]{1,0:T(8,128)S(1)}, f32[8,256]{1,0:T(8,128)S(1)}, u32[]{:S(2)}, u32[]{:S(2)}) collective-permute-start(f32[8,256]{1,0:T(8,128)S(1)} %multiply_add_fusion), channel_id=1, source_target_pairs={{0,6},{1,7},{2,4},{3,5},{4,2},{5,3},{6,0},{7,1},{8,14},{9,15},{10,... | collective-permute-start | bytes 24584 | tf_op jit(solution)/shard_map/ppermute | solution.py:28
  104.0 8.9 %collective-permute-start.37 = (f32[8,256]{1,0:T(8,128)S(1)}, f32[8,256]{1,0:T(8,128)S(1)}, u32[]{:S(2)}, u32[]{:S(2)}) collective-permute-start(f32[8,256]{1,0:T(8,128)S(1)} %multiply_add_fusion), channel_id=1, source_target_pairs={{0,4},{1,5},{2,6},{3,7},{4,0},{5,1},{6,2},{7,3},{8,12},{9,13},{10,... | collective-permute-start | bytes 24584 | tf_op jit(solution)/shard_map/ppermute | solution.py:28
  104.0 8.8 %collective-permute-start.36 = (f32[8,256]{1,0:T(8,128)S(1)}, f32[8,256]{1,0:T(8,128)S(1)}, u32[]{:S(2)}, u32[]{:S(2)}) collective-permute-start(f32[8,256]{1,0:T(8,128)S(1)} %multiply_add_fusion), channel_id=1, source_target_pairs={{0,2},{1,3},{2,0},{3,1},{4,6},{5,7},{6,4},{7,5},{8,10},{9,11},{10,... | collective-permute-start | bytes 24584 | tf_op jit(solution)/shard_map/ppermute | solution.py:28
  109.3 6.6 %collective-permute-start.32 = (f32[264,128]{1,0:T(8,128)S(1)}, f32[264,128]{1,0:T(8,128)S(1)}, u32[]{:S(2)}, u32[]{:S(2)}) collective-permute-start(f32[264,128]{1,0:T(8,128)S(1)} %get-tuple-element.53), channel_id=1, source_target_pairs={{0,2},{1,3},{2,0},{3,1},{4,6},{5,7},{6,4},{7,5},{8,10},{9,11},{10,... | collective-permute-start | bytes 405512 | tf_op jit(solution)/shard_map/ppermute | solution.py:28
  109.4 8.1 %collective-permute-start.33 = (f32[264,128]{1,0:T(8,128)S(1)}, f32[264,128]{1,0:T(8,128)S(1)}, u32[]{:S(2)}, u32[]{:S(2)}) collective-permute-start(f32[264,128]{1,0:T(8,128)S(1)} %get-tuple-element.54), channel_id=1, source_target_pairs={{0,4},{1,5},{2,6},{3,7},{4,0},{5,1},{6,2},{7,3},{8,12},{9,13},{10,... | collective-permute-start | bytes 405512 | tf_op jit(solution)/shard_map/ppermute | solution.py:28
  110.0 7.5 %collective-permute-start.34 = (f32[264,128]{1,0:T(8,128)S(1)}, f32[264,128]{1,0:T(8,128)S(1)}, u32[]{:S(2)}, u32[]{:S(2)}) collective-permute-start(f32[264,128]{1,0:T(8,128)S(1)} %get-tuple-element.55), channel_id=1, source_target_pairs={{0,6},{1,7},{2,4},{3,5},{4,2},{5,3},{6,0},{7,1},{8,14},{9,15},{10,... | collective-permute-start | bytes 405512 | tf_op jit(solution)/shard_map/ppermute | solution.py:28
  (22 other events, 71.4 us)

commit v3 on v2

v3 whole, which is shorter than its diff:
```python
import functools
import math

import jax
import jax.numpy as jnp
from jax import lax
from jax.experimental import pallas as pl
from jax.experimental.pallas import tpu as pltpu
from jax.sharding import PartitionSpec as P

ITERS = 4
EPSILON = 0.1
UNIT = 1.0 / (EPSILON * math.log(2.0))
FLOOR = -1e30
LANES = 128
GROUP = 8
MOVE_GROUP = 4

SMEM = pl.BlockSpec(memory_space=pltpu.SMEM)
VMEM = pl.BlockSpec(memory_space=pltpu.VMEM)
PARAMS = pltpu.CompilerParams(vmem_limit_bytes=40 * 1024 * 1024)


def f32(*shape):
    return jax.ShapeDtypeStruct(shape, jnp.float32)


def swap(part, axis, mask):
    return lax.ppermute(part, axis, [(i, i ^ mask) for i in range(lax.axis_size(axis))])


def near_count(axis):
    return lax.axis_size(axis) // 4


def merge_lse(parts):
    top = functools.reduce(jnp.maximum, parts)
    return top + jnp.log2(sum(jnp.exp2(part - top) for part in parts))


def exchange_lse(part, axis):
    near = near_count(axis)
    if near > 1:
        part = merge_lse([part] + [swap(part, axis, d) for d in range(1, near)])
    return [part] + [swap(part, axis, near * k) for k in range(1, 4)]


def gather_points(x_piece, y_piece, y_rows):
    nx, ny = near_count("tgt"), near_count("src")
    y_one, y_three = swap(y_piece, "src", ny), swap(y_piece, "src", 3 * ny)
    x_far = [swap(x_piece, "tgt", nx * k) for k in range(1, 4)]
    y_one, y_three, *x_far = lax.optimization_barrier((y_one, y_three, *x_far))
    half = y_rows // 2
    y_found = [
        (0, 0, y_piece),
        (ny, 0, y_one),
        (3 * ny, 0, y_three),
        (2 * ny, 0, swap(y_three[:half], "src", ny)),
        (2 * ny, half, swap(y_one[half:], "src", 3 * ny)),
    ]
    x_found = [(0, 0, x_piece)] + [(nx * k, 0, x_far[k - 1]) for k in range(1, 4)]
    return spread_near(x_found, "tgt"), spread_near(y_found, "src")


def spread_near(found, axis):
    near = near_count(axis)
    arrays = [array for _, _, array in found]
    parts = [(mask, first, k, 0, array.shape[0]) for k, (mask, first, array) in enumerate(found)]
    if near > 1:
        whole = jnp.concatenate(arrays)
        starts = [sum(a.shape[0] for a in arrays[:k]) for k in range(len(arrays))]
        arrays = [whole] + [swap(whole, axis, d) for d in range(1, near)]
        parts = [
            (mask ^ d, first, d, start, count)
            for d in range(near)
            for (mask, first, _, _, count), start in zip(parts, starts)
        ]
    return arrays, parts


def whole_block(ref, k):
    piece = ref[:, k]
    return piece.reshape(piece.shape[0] * piece.shape[1], piece.shape[2])


def split_columns(vec, split_ref):
    blocks, slots = vec.shape
    vec = vec * (1.0 / UNIT)
    parts = []
    for _ in range(3):
        part = vec.astype(jnp.bfloat16).astype(jnp.float32)
        parts.append(part)
        vec = vec - part
    parts.append(jnp.zeros((LANES - 3 * blocks, slots), jnp.float32))
    split_ref[...] = jnp.concatenate(parts, axis=0).T.astype(jnp.bfloat16)


def column_scores(stream_ref, q, split_ref, lane_ref, p):
    blocks = stream_ref.shape[1]
    lane = lax.broadcasted_iota(jnp.int32, split_ref.shape, 1)
    pick = jnp.where((lane < 3 * blocks) & (lax.rem(lane, blocks) == q), 1.0, 0.0).astype(jnp.bfloat16)
    score = lax.dot_general(
        jnp.concatenate([whole_block(stream_ref, q), split_ref[...]], axis=1),
        jnp.concatenate([whole_block(lane_ref, p), pick], axis=1),
        (((1,), (1,)), ((), ())),
        preferred_element_type=jnp.float32,
    )
    return score, jnp.max(score, axis=0, keepdims=True)


def column_lse(*operands):
    score, peak = column_scores(*operands)
    return peak * UNIT, jnp.sum(jnp.exp2((score - peak) * UNIT), axis=0, keepdims=True)


def clear(peak_ref, sum_ref):
    peak_ref[...] = jnp.full(peak_ref.shape, FLOOR, jnp.float32)
    sum_ref[...] = jnp.zeros(sum_ref.shape, jnp.float32)


def merge_slots(peak_ref, sum_ref, count):
    shape = (count, peak_ref.shape[0] // count, peak_ref.shape[1])
    peak = peak_ref[...].reshape(shape)
    top = jnp.max(peak, axis=1, keepdims=True)
    total = jnp.sum(sum_ref[...].reshape(shape) * jnp.exp2(peak - top), axis=1)
    return top[:, 0] + jnp.log2(jnp.maximum(total, 1.0))


def visit_pairs(count_ref, list_ref, tb, group, work):
    count = count_ref[0]

    @pl.loop(0, pl.cdiv(count, group))
    def _(step):
        places = [step * group + k for k in range(group)]
        codes = [list_ref[place] for place in places]
        work([(code // tb, lax.rem(code, tb), place < count) for place, code in zip(places, codes)])


def sweep(count_ref, list_ref, x_ref, y_ref, u, h, rows_ref, cols_ref, scratch):
    u_split_ref, h_split_ref, rpeak_ref, rsum_ref, cpeak_ref, csum_ref = scratch
    sb, tb = x_ref.shape[1], y_ref.shape[1]
    split_columns(u, u_split_ref)
    split_columns(h, h_split_ref)
    clear(rpeak_ref, rsum_ref)
    clear(cpeak_ref, csum_ref)

    def work(pairs):
        found = []
        for p, q, _ in pairs:
            row = column_lse(y_ref, q, h_split_ref, x_ref, p)
            col = column_lse(x_ref, p, u_split_ref, y_ref, q)
            found.append((p, q, row, col))
        for p, q, row, col in found:
            rpeak_ref[pl.ds(p * tb + q, 1), :], rsum_ref[pl.ds(p * tb + q, 1), :] = row
            cpeak_ref[pl.ds(q * sb + p, 1), :], csum_ref[pl.ds(q * sb + p, 1), :] = col

    visit_pairs(count_ref, list_ref, tb, GROUP, work)
    rows_ref[...] = merge_slots(rpeak_ref, rsum_ref, sb)
    cols_ref[...] = merge_slots(cpeak_ref, csum_ref, tb)


def sweep_scratch(sb, tb, blk):
    return [
        pltpu.VMEM((blk, LANES), jnp.bfloat16),
        pltpu.VMEM((blk, LANES), jnp.bfloat16),
        pltpu.VMEM((sb * tb, blk), jnp.float32),
        pltpu.VMEM((sb * tb, blk), jnp.float32),
        pltpu.VMEM((sb * tb, blk), jnp.float32),
        pltpu.VMEM((sb * tb, blk), jnp.float32),
    ]


def project_scratch(sb, tb, blk, width):
    return [
        pltpu.VMEM((blk, LANES), jnp.bfloat16),
        pltpu.VMEM((tb, width, blk), jnp.bfloat16),
        pltpu.VMEM((sb + 1, 1, blk), jnp.float32),
        pltpu.VMEM((sb + 1, 1, blk), jnp.float32),
        pltpu.VMEM((sb + 1, width, blk), jnp.float32),
        pltpu.VMEM((sb, blk, width), jnp.float32),
    ]


def list_kernel(keep_ref, count_ref, list_ref):
    sb, tb = keep_ref.shape

    n, last = jnp.int32(0), jnp.int32(0)
    for code in range(sb * tb):
        kept = keep_ref[code // tb, code % tb] > 0
        list_ref[n] = code
        n = n + kept.astype(jnp.int32)
        last = jnp.where(kept, code, last)
    for k in range(GROUP):
        list_ref[n + k] = last
    count_ref[0] = n


def assemble(place, counts_ref, parts, part_refs, points_ref, vec_ref):
    n, blocks, piece, width = points_ref.shape
    blk = n * piece
    vec_ref[...] = jnp.zeros(vec_ref.shape, jnp.float32)
    for mask, first, k, start, count in parts:
        owner = jnp.bitwise_xor(place, mask)
        rows = min(count, blocks * piece - first)
        points_ref[owner, first // piece : (first + rows) // piece] = part_refs[k][start : start + rows].reshape(
            rows // piece, piece, width
        )
        if rows < count:
            vecs = part_refs[k][start + rows : start + count].astype(jnp.float32)
            tile = owner * piece // LANES
            vec_ref[0, tile] += vecs[:blocks]
            vec_ref[1, tile] += vecs[blocks:]
    mass = jnp.concatenate([vec_ref[0, t] for t in range(blk // LANES)], axis=1)
    potential = jnp.concatenate([vec_ref[1, t] for t in range(blk // LANES)], axis=1) * UNIT
    block_of = lax.broadcasted_iota(jnp.int32, (blocks, blk), 0)
    slot_of = lax.broadcasted_iota(jnp.int32, (blocks, blk), 1)
    half = jnp.zeros((blocks, blk), jnp.float32)
    count = jnp.zeros((blocks, blk), jnp.int32)
    ones = jnp.ones((blocks, width), jnp.bfloat16)
    for k in range(blocks):
        wide = whole_block(points_ref, k).astype(jnp.float32)
        square = wide * wide
        high = square.astype(jnp.bfloat16)
        low = (square - high.astype(jnp.float32)).astype(jnp.bfloat16)
        norm = sum(
            lax.dot_general(ones, part, (((1,), (1,)), ((), ())), preferred_element_type=jnp.float32)
            for part in (high, low)
        )
        half = jnp.where(block_of == k, norm * (0.5 * UNIT), half)
        count = jnp.where(block_of == k, counts_ref[k], count)
    base = jnp.where(slot_of < count, jnp.log2(mass) - half, FLOOR)
    return potential, half, base


def first_kernel(x_parts, y_parts, src_counts_ref, tgt_counts_ref, count_ref, list_ref, *refs):
    nx = 1 + max(part[2] for part in x_parts)
    ny = 1 + max(part[2] for part in y_parts)
    x_in, y_in, refs = refs[:nx], refs[nx : nx + ny], refs[nx + ny :]
    x_ref, y_ref, fixed_ref, f_ref, g_ref, rows_ref, cols_ref, xvec_ref, yvec_ref = refs[:9]
    f, x_half, x_base = assemble(lax.axis_index("tgt"), src_counts_ref, x_parts, x_in, x_ref, xvec_ref)
    g, y_half, y_base = assemble(lax.axis_index("src"), tgt_counts_ref, y_parts, y_in, y_ref, yvec_ref)
    f_ref[...] = f
    g_ref[...] = g
    for k, vec in enumerate((x_half, x_base, y_half, y_base)):
        fixed_ref[k] = vec
    sweep(count_ref, list_ref, x_ref, y_ref, f + x_base, g + y_base, rows_ref, cols_ref, refs[9:])


def updated(old, half, part_refs):
    return 0.5 * (old + (half - merge_lse([ref[...] for ref in part_refs])))


def step_kernel(count_ref, list_ref, x_ref, y_ref, fixed_ref, f_in_ref, g_in_ref, *refs):
    row_refs, col_refs, refs = refs[:4], refs[4:8], refs[8:]
    f_ref, g_ref, rows_ref, cols_ref = refs[:4]
    f = updated(f_in_ref[...], fixed_ref[0], row_refs)
    g = updated(g_in_ref[...], fixed_ref[2], col_refs)
    f_ref[...] = f
    g_ref[...] = g
    sweep(count_ref, list_ref, x_ref, y_ref, f + fixed_ref[1], g + fixed_ref[3], rows_ref, cols_ref, refs[4:])


def project_kernel(near, count_ref, list_ref, x_ref, y_ref, fixed_ref, g_in_ref, *refs):
    col_refs, g_ref, out_refs = refs[:4], refs[4], refs[5 : 5 + near]
    split_ref, turned_ref, peak_ref, sum_ref, acc_ref, image_ref = refs[5 + near :]
    n, sb, piece, width = x_ref.shape
    tb = y_ref.shape[1]
    blk = n * piece
    g = updated(g_in_ref[...], fixed_ref[2], col_refs)
    g_ref[...] = g
    split_columns(g + fixed_ref[3], split_ref)
    for q in range(tb):
        turned_ref[q] = whole_block(y_ref, q).T
    clear(peak_ref, sum_ref)
    acc_ref[...] = jnp.zeros(acc_ref.shape, jnp.float32)

    def move(pairs):
        found = []
        for p, q, real in pairs:
            score, peak = column_scores(y_ref, q, split_ref, x_ref, p)
            weights = jnp.exp2((score - peak) * UNIT)
            high = weights.astype(jnp.bfloat16)
            low = (weights - high.astype(jnp.float32)).astype(jnp.bfloat16)
            ys = turned_ref[q]
            moved = jnp.dot(ys, high, preferred_element_type=jnp.float32) + jnp.dot(
                ys, low, preferred_element_type=jnp.float32
            )
            found.append((jnp.where(real, p, sb), peak * UNIT, jnp.sum(weights, axis=0, keepdims=True), moved))
        for p, peak, total, moved in found:
            old = peak_ref[p]
            new = jnp.maximum(old, peak)
            before, here = jnp.exp2(old - new), jnp.exp2(peak - new)
            peak_ref[p] = new
            sum_ref[p] = sum_ref[p] * before + total * here
            acc_ref[p] = acc_ref[p] * before + moved * here

    visit_pairs(count_ref, list_ref, tb, MOVE_GROUP, move)
    rows = []
    for p in range(sb):
        total = jnp.maximum(sum_ref[p], 1.0)
        image_ref[p] = (acc_ref[p] / total).T
        rows.append(peak_ref[p] + jnp.log2(total))
    lse = jnp.concatenate(rows, axis=0)

    me = lax.rem(lax.axis_index("tgt"), near)
    for e, out_ref in enumerate(out_refs):
        for far in range(4):
            owner = far * near + jnp.bitwise_xor(me, e)
            for p in range(sb):
                out_ref[far, p * piece : (p + 1) * piece] = image_ref[p, pl.ds(pl.multiple_of(owner * piece, piece), piece)]
            left = lse[:, :LANES]
            for t in range(1, blk // LANES):
                left = jnp.where(owner * piece // LANES == t, lse[:, t * LANES : (t + 1) * LANES], left)
            out_ref[far, sb * piece :] = left


def merge_images(parts, offset, sb, piece, turn_ref):
    whole = merge_lse([lse for _, lse in parts])
    weights = []
    for k, (_, lse) in enumerate(parts):
        turn_ref[k] = jnp.exp2(lse - whole).T
        weights.append(turn_ref[k, pl.ds(offset, piece), :])
    images = []
    for p in range(sb):
        images.append(
            sum(
                image[p * piece : (p + 1) * piece] * weight[:, p : p + 1]
                for (image, _), weight in zip(parts, weights)
            )
        )
    return images, whole


def near_kernel(near, sb, piece, *refs):
    in_refs, out_refs, turn_ref = refs[:near], refs[near : near + 4], refs[near + 4]
    place = lax.axis_index("tgt")
    me, mine = lax.rem(place, near), place // near
    rows = sb * piece
    for d, out_ref in enumerate(out_refs):
        far = jnp.bitwise_xor(mine, d)
        offset = lax.rem((far * near + me) * piece, LANES)
        parts = [(ref[far, :rows], ref[far, rows:]) for ref in in_refs]
        images, whole = merge_images(parts, pl.multiple_of(offset, piece), sb, piece, turn_ref)
        for p in range(sb):
            out_ref[p * piece : (p + 1) * piece] = images[p]
        out_ref[rows:] = whole


def far_kernel(sb, piece, *refs):
    in_refs, out_ref, turn_ref = refs[:4], refs[4], refs[5]
    rows = sb * piece
    offset = lax.rem(lax.axis_index("tgt") * piece, LANES)
    parts = [(ref[:rows], ref[rows:]) for ref in in_refs]
    images, _ = merge_images(parts, pl.multiple_of(offset, piece), sb, piece, turn_ref)
    for p in range(sb):
        out_ref[p] = images[p]


def pack_kernel(*refs):
    for k, axis in enumerate(("tgt", "src")):
        points_ref, mass_ref, potential_ref = refs[3 * k : 3 * k + 3]
        out_ref = refs[6 + k]
        blocks, piece, width = points_ref.shape
        here = lax.rem(lax.axis_index(axis) * piece, LANES)
        slot = lax.broadcasted_iota(jnp.int32, (piece, LANES), 0)
        lane = lax.broadcasted_iota(jnp.int32, (piece, LANES), 1)
        put = jnp.where(lane == slot + here, 1.0, 0.0).astype(jnp.bfloat16)
        vecs = [jnp.dot(ref[...], put, preferred_element_type=jnp.float32) for ref in (mass_ref, potential_ref)]
        out_ref[: blocks * piece] = points_ref[...].reshape(blocks * piece, width)
        out_ref[blocks * piece :] = jnp.concatenate(vecs, axis=0).astype(jnp.bfloat16)


def on_device(
    src_points, tgt_points, src_mass, tgt_mass, src_potential, tgt_potential, src_counts, tgt_counts, keep
):
    ntgt, nsrc = lax.axis_size("tgt"), lax.axis_size("src")
    near = near_count("tgt")
    sb, src_piece, width = src_points.shape
    tb, tgt_piece, _ = tgt_points.shape
    blk = src_piece * ntgt
    count, pairs = pl.pallas_call(
        list_kernel,
        out_shape=(
            jax.ShapeDtypeStruct((1,), jnp.int32),
            jax.ShapeDtypeStruct((sb * tb + GROUP,), jnp.int32),
        ),
        in_specs=[SMEM],
        out_specs=(SMEM, SMEM),
        name="kept_pairs",
    )(keep)

    x_rows, y_rows = sb * src_piece, tb * tgt_piece
    x_packed, y_packed = pl.pallas_call(
        pack_kernel,
        out_shape=(
            jax.ShapeDtypeStruct((x_rows + 2 * sb, width), jnp.bfloat16),
            jax.ShapeDtypeStruct((y_rows + 2 * tb, width), jnp.bfloat16),
        ),
        in_specs=[VMEM] * 6,
        out_specs=(VMEM, VMEM),
        name="pack",
    )(src_points, src_mass, src_potential, tgt_points, tgt_mass, tgt_potential)
    (x_in, x_parts), (y_in, y_parts) = gather_points(x_packed, y_packed, y_rows)

    vectors = (f32(sb, blk), f32(tb, blk), f32(sb, blk), f32(tb, blk))
    x, y, fixed, f, g, rows, cols = pl.pallas_call(
        functools.partial(first_kernel, x_parts, y_parts),
        out_shape=(
            jax.ShapeDtypeStruct((ntgt, sb, src_piece, width), jnp.bfloat16),
            jax.ShapeDtypeStruct((nsrc, tb, tgt_piece, width), jnp.bfloat16),
            f32(4, sb, blk),
        )
        + vectors,
        in_specs=[SMEM] * 4 + [VMEM] * (len(x_in) + len(y_in)),
        out_specs=(VMEM,) * 7,
        scratch_shapes=[
            pltpu.VMEM((2, blk // LANES, sb, LANES), jnp.float32),
            pltpu.VMEM((2, blk // LANES, tb, LANES), jnp.float32),
        ]
        + sweep_scratch(sb, tb, blk),
        compiler_params=PARAMS,
        name="first_sweep",
    )(src_counts, tgt_counts, count, pairs, *x_in, *y_in)

    step = pl.pallas_call(
        step_kernel,
        out_shape=vectors,
        in_specs=[SMEM] * 2 + [VMEM] * 13,
        out_specs=(VMEM,) * 4,
        scratch_shapes=sweep_scratch(sb, tb, blk),
        compiler_params=PARAMS,
        name="sweep",
    )
    for _ in range(ITERS - 1):
        row_parts = exchange_lse(rows, "tgt")
        col_parts = exchange_lse(cols, "src")
        f, g, rows, cols = step(count, pairs, x, y, fixed, f, g, *row_parts, *col_parts)

    col_parts = exchange_lse(cols, "src")
    row_parts = exchange_lse(rows, "tgt")
    tile = sb * src_piece + sb
    g, *near_parts = pl.pallas_call(
        functools.partial(project_kernel, near),
        out_shape=(f32(tb, blk),) + (f32(4, tile, width),) * near,
        in_specs=[SMEM] * 2 + [VMEM] * 8,
        out_specs=(VMEM,) * (1 + near),
        scratch_shapes=project_scratch(sb, tb, blk, width),
        compiler_params=PARAMS,
        name="project",
    )(count, pairs, x, y, fixed, g, *col_parts)
    if near > 1:
        near_parts = near_parts[:1] + [swap(near_parts[d], "tgt", d) for d in range(1, near)]
    far_parts = pl.pallas_call(
        functools.partial(near_kernel, near, sb, src_piece),
        out_shape=(f32(tile, width),) * 4,
        in_specs=[VMEM] * near,
        out_specs=(VMEM,) * 4,
        scratch_shapes=[pltpu.VMEM((near, LANES, sb), jnp.float32)],
        compiler_params=PARAMS,
        name="merge_near",
    )(*near_parts)
    far_parts = [far_parts[0]] + [swap(far_parts[k], "tgt", near * k) for k in range(1, 4)]
    images = pl.pallas_call(
        functools.partial(far_kernel, sb, src_piece),
        out_shape=f32(sb, src_piece, width),
        in_specs=[VMEM] * 4,
        out_specs=VMEM,
        scratch_shapes=[pltpu.VMEM((4, LANES, sb), jnp.float32)],
        compiler_params=PARAMS,
        name="merge_far",
    )(*far_parts)

    f = 0.5 * (f + (fixed[0] - merge_lse(row_parts)))
    src_final = lax.dynamic_slice_in_dim(f * (1.0 / UNIT), lax.axis_index("tgt") * src_piece, src_piece, 1)
    tgt_final = lax.dynamic_slice_in_dim(g * (1.0 / UNIT), lax.axis_index("src") * tgt_piece, tgt_piece, 1)
    return images, src_final, tgt_final


def solution(mesh):
    return jax.shard_map(
        on_device,
        mesh=mesh,
        in_specs=(
            P("src", "tgt", None),
            P("tgt", "src", None),
            P("src", "tgt"),
            P("tgt", "src"),
            P("src", "tgt"),
            P("tgt", "src"),
            P("src"),
            P("tgt"),
            P("src", "tgt"),
        ),
        out_specs=(P("src", "tgt", None), P("src", "tgt"), P("tgt", "src")),
        check_vma=False,
    )
```

time: 118 us -> 102 us (0.86); the launches traced: 119 us -> 101 us
  Pallas kernels: 45.6 us -> 26.3 us
  local copies, waits for them, and re-layouts: 4.45 us -> 1.65 us
  waiting for transfers between devices: 21.5 us -> 24.2 us
  starting transfers between devices: 44.9 us -> 46.7 us
    pallas_call x1, Pallas kernels: 14.2 us -> 5.07 us  [on_device(): pl.pallas_call(functools.partial(project_kernel, near), out_shape=(f32(tb...]
    pallas_call x3, Pallas kernels: 19.1 us -> 11.8 us  [on_device(): step(count, pairs, x, y, fixed, f, g, *row_parts, *col_parts)]
    ppermute x39 -> x40, waiting for transfers between devices: 21.5 us -> 24.2 us  [swap(): lax.ppermute(part, axis, [(i, i ^ mask) for i in range(lax.axis_size(axis...]
    ppermute x39 -> x40, starting transfers between devices: 44.9 us -> 46.7 us  [swap(): lax.ppermute(part, axis, [(i, i ^ mask) for i in range(lax.axis_size(axis...]
    another operation x8 -> x0, local copies, waits for them, and re-layouts: 1.73 us -> none  [placed(): return jnp.where(inside, jnp.tile(vec, (1, LANES // piece)), 0)]
    unnamed x14 -> x11, local copies, waits for them, and re-layouts: 2.72 us -> 1.62 us
    pallas_call x1 -> x2, Pallas kernels: 7.06 us -> 6.37 us  [the longest x1 4.64 us: on_device(): pl.pallas_call(functools.partial(first_kernel, x_parts, y_parts), out_sha...]
  transfers between devices with their start and end apart: 39 -> 40, of which waited for: 13 -> 21; matrix products, arithmetic and copies ran while one was open for 2% -> 2% of each run, Pallas kernels for 15% -> 7%
where the time goes in v3:
time: 102 us; the launch traced here: 101 us
  starting transfers between devices  46.7 us (46%)
  Pallas kernels  26.3 us (26%)
  waiting for transfers between devices  24.2 us (24%)
  local copies, waits for them, and re-layouts  1.65 us (2%)
  other arithmetic  1.44 us (1%)
    ppermute x40, starting transfers between devices, swap(): lax.ppermute(part, axis, [(i, i ^ mask) for i in range(lax.axis_size(axis...  46.7 us
    ppermute x40, waiting for transfers between devices, swap(): lax.ppermute(part, axis, [(i, i ^ mask) for i in range(lax.axis_size(axis...  24.2 us
    pallas_call x3, Pallas kernels, on_device(): step(count, pairs, x, y, fixed, f, g, *row_parts, *col_parts)  11.8 us
    pallas_call x1, Pallas kernels, on_device(): pl.pallas_call(functools.partial(project_kernel, near), out_shape=(f32(tb...  5.07 us
    pallas_call x1, Pallas kernels, on_device(): pl.pallas_call(functools.partial(first_kernel, x_parts, y_parts), out_sha...  4.64 us
  transfers between devices with their start and end apart: 40, of which 21 were waited for; matrix products, arithmetic and copies ran while one was open for 2% of the time, Pallas kernels for 7%

profile of v3, /device:TPU:0, one launch (start us, length us, event | category | flops | bytes accessed | tf_op | source)
XLA Modules:
  0.0 101.2 jit_solution(11364948544068190321)
XLA Ops:
  0.6 1.7 %pack.1 = (bf16[272,128]{1,0:T(8,128)(2,1)}, bf16[528,128]{1,0:T(8,128)(2,1)}) custom-call(bf16[8,32,128]{2,1,0:T(8,128)(2,1)} %refs_0_.1, bf16[8,32]{1,0:T(8,128)(2,1)} %refs_1_.1, bf16[8,32]{1,0:T(8,128)(2,1)} %refs_2_.1, bf16[8,64,128]{2,1,0:T(8,128)(2,1)} %refs_3_.1, bf16[8,64]{1,0:T(8,128)(2,1)} %refs_4_.1, bf16[8,64]{1,0:T(8,128)(2,1)} %refs_5_.1), custom_call_target="tpu_custom_call" | custom-call | tf_op jit(solution)/shard_map/pack/pallas_call | solution.py:393
  2.4 5.0 %collective-permute-start.1 = (bf16[528,128]{1,0:T(8,128)(2,1)}, bf16[528,128]{1,0:T(8,128)(2,1)S(1)}, u32[]{:S(2)}, u32[]{:S(2)}) collective-permute-start(bf16[528,128]{1,0:T(8,128)(2,1)} %get-tuple-element.41.refs_2_), channel_id=1, source_target_pairs={{0,24},{8,16},{16,8},{24,0},{1,25},{9,17},{17,9},{25,1},{2,26},{10... | collective-permute-start | bytes 405512 | tf_op jit(solution)/shard_map/ppermute | solution.py:29
  7.4 2.4 %collective-permute-start.4 = (bf16[272,128]{1,0:T(8,128)(2,1)}, bf16[272,128]{1,0:T(8,128)(2,1)S(1)}, u32[]{:S(2)}, u32[]{:S(2)}) collective-permute-start(bf16[272,128]{1,0:T(8,128)(2,1)} %get-tuple-element.40), channel_id=1, source_target_pairs={{0,6},{1,7},{2,4},{3,5},{4,2},{5,3},{6,0},{7,1},{8,14},{9,15},{10,... | collective-permute-start | bytes 208904 | tf_op jit(solution)/shard_map/ppermute | solution.py:29
  18.6 3.2 %collective-permute-done.6.refs_5_ = bf16[256,128]{1,0:T(8,128)(2,1)S(1)} collective-permute-done((bf16[256,128]{1,0:T(8,128)(2,1)S(1)}, bf16[256,128]{1,0:T(8,128)(2,1)S(1)}, u32[]{:S(2)}, u32[]{:S(2)}) %collective-permute-start.6) | collective-permute-done | bytes 65568 | tf_op jit(solution)/shard_map/ppermute | solution.py:29
  22.6 4.6 %first_sweep.1 = (bf16[8,8,32,128]{3,2,1,0:T(8,128)(2,1)S(1)}, bf16[4,8,64,128]{3,2,1,0:T(8,128)(2,1)S(1)}, f32[4,8,256]{2,1,0:T(8,128)S(1)}, f32[8,256]{1,0:T(8...) custom-call(s32[8]{0:T(128)S(1)} %copy-done.2, s32[8]{0:T(128)S(1)} %copy-done.3, ...), custom_call_target="tpu_custom_call" | custom-call | tf_op jit(solution)/shard_map/first_sweep/pallas_call | solution.py:406
  27.4 3.2 %collective-permute-start.14 = (f32[8,256]{1,0:T(8,128)S(1)}, f32[8,256]{1,0:T(8,128)S(1)}, u32[]{:S(2)}, u32[]{:S(2)}) collective-permute-start(f32[8,256]{1,0:T(8,128)S(1)} %get-tuple-element.53.refs_4_), channel_id=1, source_target_pairs={{0,24},{8,16},{16,8},{24,0},{1,25},{9,17},{17,9},{25,1},{2,26},{10... | collective-permute-start | bytes 24584 | tf_op jit(solution)/shard_map/ppermute | solution.py:29
  31.8 2.3 %collective-permute-start.11 = (f32[8,256]{1,0:T(8,128)S(1)}, f32[8,256]{1,0:T(8,128)S(1)}, u32[]{:S(2)}, u32[]{:S(2)}) collective-permute-start(f32[8,256]{1,0:T(8,128)S(1)} %multiply_add_fusion.3.refs_0_), channel_id=1, source_target_pairs={{0,6},{1,7},{2,4},{3,5},{4,2},{5,3},{6,0},{7,1},{8,14},{9,15},{10,... | collective-permute-start | bytes 24584 | tf_op jit(solution)/shard_map/ppermute | solution.py:29
  38.0 3.9 %sweep.3 = (f32[8,256]{1,0:T(8,128)S(1)}, f32[8,256]{1,0:T(8,128)S(1)}, f32[8,256]{1,0:T(8,128)S(1)}, f32[8,256]{1,0:T(8,128)S(1)}) custom-call(s32[1]{0:T(128)} %get-tuple-element.38.count_ref, s32[72]{0:T(128)S(1)} %copy-done.1, bf16[8,8,32,128]{3,2,1,0:T(8,128)(2,1)S(1)} %get-tuple-element.47.x_ref, bf16[4,8,64,128]{3,2,1,0:T(8,128)(2,1)S(1)} %get-tuple-element.48.y_ref, ...), custom_call_target="tpu_custom_call" | custom-call | tf_op jit(solution)/shard_map/sweep/pallas_call | solution.py:437
  42.0 3.8 %collective-permute-start.21 = (f32[8,256]{1,0:T(8,128)S(1)}, f32[8,256]{1,0:T(8,128)S(1)}, u32[]{:S(2)}, u32[]{:S(2)}) collective-permute-start(f32[8,256]{1,0:T(8,128)S(1)} %get-tuple-element.57.refs_4_), channel_id=1, source_target_pairs={{0,24},{8,16},{16,8},{24,0},{1,25},{9,17},{17,9},{25,1},{2,26},{10... | collective-permute-start | bytes 24584 | tf_op jit(solution)/shard_map/ppermute | solution.py:29
  46.5 2.3 %collective-permute-start.18 = (f32[8,256]{1,0:T(8,128)S(1)}, f32[8,256]{1,0:T(8,128)S(1)}, u32[]{:S(2)}, u32[]{:S(2)}) collective-permute-start(f32[8,256]{1,0:T(8,128)S(1)} %multiply_add_fusion.2.refs_0_), channel_id=1, source_target_pairs={{0,6},{1,7},{2,4},{3,5},{4,2},{5,3},{6,0},{7,1},{8,14},{9,15},{10,... | collective-permute-start | bytes 24584 | tf_op jit(solution)/shard_map/ppermute | solution.py:29
  53.4 3.9 %sweep.4 = (f32[8,256]{1,0:T(8,128)S(1)}, f32[8,256]{1,0:T(8,128)S(1)}, f32[8,256]{1,0:T(8,128)S(1)}, f32[8,256]{1,0:T(8,128)S(1)}) custom-call(s32[1]{0:T(128)} %get-tuple-element.38.count_ref, s32[72]{0:T(128)S(1)} %copy-done.1, bf16[8,8,32,128]{3,2,1,0:T(8,128)(2,1)S(1)} %get-tuple-element.47.x_ref, bf16[4,8,64,128]{3,2,1,0:T(8,128)(2,1)S(1)} %get-tuple-element.48.y_ref, ...), custom_call_target="tpu_custom_call" | custom-call | tf_op jit(solution)/shard_map/sweep/pallas_call | solution.py:437
  57.4 3.8 %collective-permute-start.28 = (f32[8,256]{1,0:T(8,128)S(1)}, f32[8,256]{1,0:T(8,128)S(1)}, u32[]{:S(2)}, u32[]{:S(2)}) collective-permute-start(f32[8,256]{1,0:T(8,128)S(1)} %get-tuple-element.61.refs_4_), channel_id=1, source_target_pairs={{0,24},{8,16},{16,8},{24,0},{1,25},{9,17},{17,9},{25,1},{2,26},{10... | collective-permute-start | bytes 24584 | tf_op jit(solution)/shard_map/ppermute | solution.py:29
  61.9 2.6 %collective-permute-start.25 = (f32[8,256]{1,0:T(8,128)S(1)}, f32[8,256]{1,0:T(8,128)S(1)}, u32[]{:S(2)}, u32[]{:S(2)}) collective-permute-start(f32[8,256]{1,0:T(8,128)S(1)} %multiply_add_fusion.1.refs_0_), channel_id=1, source_target_pairs={{0,6},{1,7},{2,4},{3,5},{4,2},{5,3},{6,0},{7,1},{8,14},{9,15},{10,... | collective-permute-start | bytes 24584 | tf_op jit(solution)/shard_map/ppermute | solution.py:29
  66.5 1.7 %collective-permute-done.24.refs_2_ = f32[8,256]{1,0:T(8,128)S(1)} collective-permute-done((f32[8,256]{1,0:T(8,128)S(1)}, f32[8,256]{1,0:T(8,128)S(1)}, u32[]{:S(2)}, u32[]{:S(2)}) %collective-permute-start.24) | collective-permute-done | bytes 8224 | tf_op jit(solution)/shard_map/ppermute | solution.py:29
  68.6 3.9 %sweep.5 = (f32[8,256]{1,0:T(8,128)S(1)}, f32[8,256]{1,0:T(8,128)S(1)}, f32[8,256]{1,0:T(8,128)S(1)}, f32[8,256]{1,0:T(8,128)S(1)}) custom-call(s32[1]{0:T(128)} %get-tuple-element.38.count_ref, s32[72]{0:T(128)S(1)} %copy-done.1, bf16[8,8,32,128]{3,2,1,0:T(8,128)(2,1)S(1)} %get-tuple-element.47.x_ref, bf16[4,8,64,128]{3,2,1,0:T(8,128)(2,1)S(1)} %get-tuple-element.48.y_ref, ...), custom_call_target="tpu_custom_call" | custom-call | tf_op jit(solution)/shard_map/sweep/pallas_call | solution.py:437
  72.6 3.8 %collective-permute-start.31 = (f32[8,256]{1,0:T(8,128)S(1)}, f32[8,256]{1,0:T(8,128)S(1)}, u32[]{:S(2)}, u32[]{:S(2)}) collective-permute-start(f32[8,256]{1,0:T(8,128)S(1)} %get-tuple-element.63.refs_0_), channel_id=1, source_target_pairs={{0,24},{8,16},{16,8},{24,0},{1,25},{9,17},{17,9},{25,1},{2,26},{10... | collective-permute-start | bytes 24584 | tf_op jit(solution)/shard_map/ppermute | solution.py:29
  78.1 2.8 %collective-permute-done.30.refs_2_ = f32[8,256]{1,0:T(8,128)S(1)} collective-permute-done((f32[8,256]{1,0:T(8,128)S(1)}, f32[8,256]{1,0:T(8,128)S(1)}, u32[]{:S(2)}, u32[]{:S(2)}) %collective-permute-start.30) | collective-permute-done | bytes 8224 | tf_op jit(solution)/shard_map/ppermute | solution.py:29
  80.9 5.1 %project.1 = (f32[8,256]{1,0:T(8,128)S(1)}, f32[4,264,128]{2,1,0:T(8,128)S(1)}, f32[4,264,128]{2,1,0:T(8,128)S(1)}) custom-call(s32[1]{0:T(128)} %get-tuple-element.38.count_ref, s32[72]{0:T(128)S(1)} %copy-done.1, bf16[8,8,32,128]{3,2,1,0:T(8,128)(2,1)S(1)} %get-tuple-element.47.x_ref, bf16[4,8,64,128]{3,2,1,0:T(8,128)(2,1)S(1)} %get-tuple-element.48.y_ref, ...), custom_call_target="tpu_custom_call" | custom-call | tf_op jit(solution)/shard_map/project/pallas_call | solution.py:442
  86.2 1.5 %collective-permute-start.39 = (f32[8,256]{1,0:T(8,128)S(1)}, f32[8,256]{1,0:T(8,128)S(1)}, u32[]{:S(2)}, u32[]{:S(2)}) collective-permute-start(f32[8,256]{1,0:T(8,128)S(1)} %multiply_add_fusion), channel_id=1, source_target_pairs={{0,6},{1,7},{2,4},{3,5},{4,2},{5,3},{6,0},{7,1},{8,14},{9,15},{10,... | collective-permute-start | bytes 24584 | tf_op jit(solution)/shard_map/ppermute | solution.py:29
  87.9 1.9 %collective-permute-start.37 = (f32[8,256]{1,0:T(8,128)S(1)}, f32[8,256]{1,0:T(8,128)S(1)}, u32[]{:S(2)}, u32[]{:S(2)}) collective-permute-start(f32[8,256]{1,0:T(8,128)S(1)} %multiply_add_fusion), channel_id=1, source_target_pairs={{0,2},{1,3},{2,0},{3,1},{4,6},{5,7},{6,4},{7,5},{8,10},{9,11},{10,... | collective-permute-start | bytes 24584 | tf_op jit(solution)/shard_map/ppermute | solution.py:29
  91.3 1.9 %collective-permute-start.34 = (f32[264,128]{1,0:T(8,128)S(1)}, f32[264,128]{1,0:T(8,128)S(1)}, u32[]{:S(2)}, u32[]{:S(2)}) collective-permute-start(f32[264,128]{1,0:T(8,128)S(1)} %get-tuple-element.68), channel_id=1, source_target_pairs={{0,4},{1,5},{2,6},{3,7},{4,0},{5,1},{6,2},{7,3},{8,12},{9,13},{10,... | collective-permute-start | bytes 405512 | tf_op jit(solution)/shard_map/ppermute | solution.py:29
  93.1 1.4 %collective-permute-start.35 = (f32[264,128]{1,0:T(8,128)S(1)}, f32[264,128]{1,0:T(8,128)S(1)}, u32[]{:S(2)}, u32[]{:S(2)}) collective-permute-start(f32[264,128]{1,0:T(8,128)S(1)} %get-tuple-element.69), channel_id=1, source_target_pairs={{0,6},{1,7},{2,4},{3,5},{4,2},{5,3},{6,0},{7,1},{8,14},{9,15},{10,... | collective-permute-start | bytes 405512 | tf_op jit(solution)/shard_map/ppermute | solution.py:29
  95.3 2.3 %collective-permute-done.33.refs_1_ = f32[264,128]{1,0:T(8,128)S(1)} collective-permute-done((f32[264,128]{1,0:T(8,128)S(1)}, f32[264,128]{1,0:T(8,128)S(1)}, u32[]{:S(2)}, u32[]{:S(2)}) %collective-permute-start.33) | collective-permute-done | bytes 135200 | tf_op jit(solution)/shard_map/ppermute | solution.py:29
  98.4 1.7 %collective-permute-done.35.refs_3_ = f32[264,128]{1,0:T(8,128)S(1)} collective-permute-done((f32[264,128]{1,0:T(8,128)S(1)}, f32[264,128]{1,0:T(8,128)S(1)}, u32[]{:S(2)}, u32[]{:S(2)}) %collective-permute-start.35) | collective-permute-done | bytes 135200 | tf_op jit(solution)/shard_map/ppermute | solution.py:29
  (87 shorter events, 29.3 us)
Async XLA Ops:
  2.4 12.5 %collective-permute-start.1 = (bf16[528,128]{1,0:T(8,128)(2,1)}, bf16[528,128]{1,0:T(8,128)(2,1)S(1)}, u32[]{:S(2)}, u32[]{:S(2)}) collective-permute-start(bf16[528,128]{1,0:T(8,128)(2,1)} %get-tuple-element.41.refs_2_), channel_id=1, source_target_pairs={{0,24},{8,16},{16,8},{24,0},{1,25},{9,17},{17,9},{25,1},{2,26},{10... | collective-permute-start | bytes 405512 | tf_op jit(solution)/shard_map/ppermute | solution.py:29
  7.4 7.5 %collective-permute-start = (bf16[528,128]{1,0:T(8,128)(2,1)}, bf16[528,128]{1,0:T(8,128)(2,1)S(1)}, u32[]{:S(2)}, u32[]{:S(2)}) collective-permute-start(bf16[528,128]{1,0:T(8,128)(2,1)} %get-tuple-element.41.refs_2_), channel_id=1, source_target_pairs={{0,8},{8,0},{16,24},{24,16},{1,9},{9,1},{17,25},{25,17},{2,10},{10... | collective-permute-start | bytes 405512 | tf_op jit(solution)/shard_map/ppermute | solution.py:29
  7.4 5.5 %collective-permute-start.4 = (bf16[272,128]{1,0:T(8,128)(2,1)}, bf16[272,128]{1,0:T(8,128)(2,1)S(1)}, u32[]{:S(2)}, u32[]{:S(2)}) collective-permute-start(bf16[272,128]{1,0:T(8,128)(2,1)} %get-tuple-element.40), channel_id=1, source_target_pairs={{0,6},{1,7},{2,4},{3,5},{4,2},{5,3},{6,0},{7,1},{8,14},{9,15},{10,... | collective-permute-start | bytes 208904 | tf_op jit(solution)/shard_map/ppermute | solution.py:29
  15.0 7.0 %collective-permute-start.5 = (bf16[1088,128]{1,0:T(8,128)(2,1)S(1)}, bf16[1088,128]{1,0:T(8,128)(2,1)S(1)}, u32[]{:S(2)}, u32[]{:S(2)}) collective-permute-start(bf16[1088,128]{1,0:T(8,128)(2,1)S(1)} %constant_dynamic-update-slice_fusion.refs_0_), channel_id=1, source_target_pairs={{0,1},{1,0},{2,3},{3,2},{4,5},{5,4},{6,7},{7,6},{8,9},{9,8},{10,11... | collective-permute-start | bytes 835592 | tf_op jit(solution)/shard_map/ppermute | solution.py:29
  15.1 6.9 %collective-permute-start.7 = (bf16[272,128]{1,0:T(8,128)(2,1)S(1)}, bf16[272,128]{1,0:T(8,128)(2,1)S(1)}, u32[]{:S(2)}, u32[]{:S(2)}) collective-permute-start(bf16[272,128]{1,0:T(8,128)(2,1)S(1)} %slice.10), channel_id=1, source_target_pairs={{0,24},{8,16},{16,8},{24,0},{1,25},{9,17},{17,9},{25,1},{2,26},{10... | collective-permute-start | bytes 208904 | tf_op jit(solution)/shard_map/ppermute | solution.py:29
  16.1 5.7 %collective-permute-start.6 = (bf16[256,128]{1,0:T(8,128)(2,1)S(1)}, bf16[256,128]{1,0:T(8,128)(2,1)S(1)}, u32[]{:S(2)}, u32[]{:S(2)}) collective-permute-start(bf16[256,128]{1,0:T(8,128)(2,1)S(1)} %slice.9), channel_id=1, source_target_pairs={{0,8},{8,0},{16,24},{24,16},{1,9},{9,1},{17,25},{25,17},{2,10},{10... | collective-permute-start | bytes 196616 | tf_op jit(solution)/shard_map/ppermute | solution.py:29
  27.4 7.0 %collective-permute-start.14 = (f32[8,256]{1,0:T(8,128)S(1)}, f32[8,256]{1,0:T(8,128)S(1)}, u32[]{:S(2)}, u32[]{:S(2)}) collective-permute-start(f32[8,256]{1,0:T(8,128)S(1)} %get-tuple-element.53.refs_4_), channel_id=1, source_target_pairs={{0,24},{8,16},{16,8},{24,0},{1,25},{9,17},{17,9},{25,1},{2,26},{10... | collective-permute-start | bytes 24584 | tf_op jit(solution)/shard_map/ppermute | solution.py:29
  30.5 4.9 %collective-permute-start.13 = (f32[8,256]{1,0:T(8,128)S(1)}, f32[8,256]{1,0:T(8,128)S(1)}, u32[]{:S(2)}, u32[]{:S(2)}) collective-permute-start(f32[8,256]{1,0:T(8,128)S(1)} %get-tuple-element.53.refs_4_), channel_id=1, source_target_pairs={{0,16},{8,24},{16,0},{24,8},{1,17},{9,25},{17,1},{25,9},{2,18},{10... | collective-permute-start | bytes 24584 | tf_op jit(solution)/shard_map/ppermute | solution.py:29
  30.5 4.9 %collective-permute-start.12 = (f32[8,256]{1,0:T(8,128)S(1)}, f32[8,256]{1,0:T(8,128)S(1)}, u32[]{:S(2)}, u32[]{:S(2)}) collective-permute-start(f32[8,256]{1,0:T(8,128)S(1)} %get-tuple-element.53.refs_4_), channel_id=1, source_target_pairs={{0,8},{8,0},{16,24},{24,16},{1,9},{9,1},{17,25},{25,17},{2,10},{10... | collective-permute-start | bytes 24584 | tf_op jit(solution)/shard_map/ppermute | solution.py:29
  31.8 4.6 %collective-permute-start.11 = (f32[8,256]{1,0:T(8,128)S(1)}, f32[8,256]{1,0:T(8,128)S(1)}, u32[]{:S(2)}, u32[]{:S(2)}) collective-permute-start(f32[8,256]{1,0:T(8,128)S(1)} %multiply_add_fusion.3.refs_0_), channel_id=1, source_target_pairs={{0,6},{1,7},{2,4},{3,5},{4,2},{5,3},{6,0},{7,1},{8,14},{9,15},{10,... | collective-permute-start | bytes 24584 | tf_op jit(solution)/shard_map/ppermute | solution.py:29
  42.0 7.7 %collective-permute-start.21 = (f32[8,256]{1,0:T(8,128)S(1)}, f32[8,256]{1,0:T(8,128)S(1)}, u32[]{:S(2)}, u32[]{:S(2)}) collective-permute-start(f32[8,256]{1,0:T(8,128)S(1)} %get-tuple-element.57.refs_4_), channel_id=1, source_target_pairs={{0,24},{8,16},{16,8},{24,0},{1,25},{9,17},{17,9},{25,1},{2,26},{10... | collective-permute-start | bytes 24584 | tf_op jit(solution)/shard_map/ppermute | solution.py:29
  45.8 4.5 %collective-permute-start.20 = (f32[8,256]{1,0:T(8,128)S(1)}, f32[8,256]{1,0:T(8,128)S(1)}, u32[]{:S(2)}, u32[]{:S(2)}) collective-permute-start(f32[8,256]{1,0:T(8,128)S(1)} %get-tuple-element.57.refs_4_), channel_id=1, source_target_pairs={{0,16},{8,24},{16,0},{24,8},{1,17},{9,25},{17,1},{25,9},{2,18},{10... | collective-permute-start | bytes 24584 | tf_op jit(solution)/shard_map/ppermute | solution.py:29
  46.5 4.6 %collective-permute-start.18 = (f32[8,256]{1,0:T(8,128)S(1)}, f32[8,256]{1,0:T(8,128)S(1)}, u32[]{:S(2)}, u32[]{:S(2)}) collective-permute-start(f32[8,256]{1,0:T(8,128)S(1)} %multiply_add_fusion.2.refs_0_), channel_id=1, source_target_pairs={{0,6},{1,7},{2,4},{3,5},{4,2},{5,3},{6,0},{7,1},{8,14},{9,15},{10,... | collective-permute-start | bytes 24584 | tf_op jit(solution)/shard_map/ppermute | solution.py:29
  57.3 4.6 %collective-permute-start.22 = (f32[8,256]{1,0:T(8,128)S(1)}, f32[8,256]{1,0:T(8,128)S(1)}, u32[]{:S(2)}, u32[]{:S(2)}) collective-permute-start(f32[8,256]{1,0:T(8,128)S(1)} %get-tuple-element.60), channel_id=1, source_target_pairs={{0,1},{1,0},{2,3},{3,2},{4,5},{5,4},{6,7},{7,6},{8,9},{9,8},{10,11... | collective-permute-start | bytes 24584 | tf_op jit(solution)/shard_map/ppermute | solution.py:29
  57.4 7.6 %collective-permute-start.28 = (f32[8,256]{1,0:T(8,128)S(1)}, f32[8,256]{1,0:T(8,128)S(1)}, u32[]{:S(2)}, u32[]{:S(2)}) collective-permute-start(f32[8,256]{1,0:T(8,128)S(1)} %get-tuple-element.61.refs_4_), channel_id=1, source_target_pairs={{0,24},{8,16},{16,8},{24,0},{1,25},{9,17},{17,9},{25,1},{2,26},{10... | collective-permute-start | bytes 24584 | tf_op jit(solution)/shard_map/ppermute | solution.py:29
  61.9 4.6 %collective-permute-start.25 = (f32[8,256]{1,0:T(8,128)S(1)}, f32[8,256]{1,0:T(8,128)S(1)}, u32[]{:S(2)}, u32[]{:S(2)}) collective-permute-start(f32[8,256]{1,0:T(8,128)S(1)} %multiply_add_fusion.1.refs_0_), channel_id=1, source_target_pairs={{0,6},{1,7},{2,4},{3,5},{4,2},{5,3},{6,0},{7,1},{8,14},{9,15},{10,... | collective-permute-start | bytes 24584 | tf_op jit(solution)/shard_map/ppermute | solution.py:29
  72.6 5.5 %collective-permute-start.31 = (f32[8,256]{1,0:T(8,128)S(1)}, f32[8,256]{1,0:T(8,128)S(1)}, u32[]{:S(2)}, u32[]{:S(2)}) collective-permute-start(f32[8,256]{1,0:T(8,128)S(1)} %get-tuple-element.63.refs_0_), channel_id=1, source_target_pairs={{0,24},{8,16},{16,8},{24,0},{1,25},{9,17},{17,9},{25,1},{2,26},{10... | collective-permute-start | bytes 24584 | tf_op jit(solution)/shard_map/ppermute | solution.py:29
  77.0 9.1 %collective-permute-start.36 = (f32[8,256]{1,0:T(8,128)S(1)}, f32[8,256]{1,0:T(8,128)S(1)}, u32[]{:S(2)}, u32[]{:S(2)}) collective-permute-start(f32[8,256]{1,0:T(8,128)S(1)} %get-tuple-element.71), channel_id=1, source_target_pairs={{0,1},{1,0},{2,3},{3,2},{4,5},{5,4},{6,7},{7,6},{8,9},{9,8},{10,11... | collective-permute-start | bytes 24584 | tf_op jit(solution)/shard_map/ppermute | solution.py:29
  86.2 7.0 %collective-permute-start.39 = (f32[8,256]{1,0:T(8,128)S(1)}, f32[8,256]{1,0:T(8,128)S(1)}, u32[]{:S(2)}, u32[]{:S(2)}) collective-permute-start(f32[8,256]{1,0:T(8,128)S(1)} %multiply_add_fusion), channel_id=1, source_target_pairs={{0,6},{1,7},{2,4},{3,5},{4,2},{5,3},{6,0},{7,1},{8,14},{9,15},{10,... | collective-permute-start | bytes 24584 | tf_op jit(solution)/shard_map/ppermute | solution.py:29
  87.7 6.9 %collective-permute-start.38 = (f32[8,256]{1,0:T(8,128)S(1)}, f32[8,256]{1,0:T(8,128)S(1)}, u32[]{:S(2)}, u32[]{:S(2)}) collective-permute-start(f32[8,256]{1,0:T(8,128)S(1)} %multiply_add_fusion), channel_id=1, source_target_pairs={{0,4},{1,5},{2,6},{3,7},{4,0},{5,1},{6,2},{7,3},{8,12},{9,13},{10,... | collective-permute-start | bytes 24584 | tf_op jit(solution)/shard_map/ppermute | solution.py:29
  87.9 6.7 %collective-permute-start.37 = (f32[8,256]{1,0:T(8,128)S(1)}, f32[8,256]{1,0:T(8,128)S(1)}, u32[]{:S(2)}, u32[]{:S(2)}) collective-permute-start(f32[8,256]{1,0:T(8,128)S(1)} %multiply_add_fusion), channel_id=1, source_target_pairs={{0,2},{1,3},{2,0},{3,1},{4,6},{5,7},{6,4},{7,5},{8,10},{9,11},{10,... | collective-permute-start | bytes 24584 | tf_op jit(solution)/shard_map/ppermute | solution.py:29
  91.0 6.6 %collective-permute-start.33 = (f32[264,128]{1,0:T(8,128)S(1)}, f32[264,128]{1,0:T(8,128)S(1)}, u32[]{:S(2)}, u32[]{:S(2)}) collective-permute-start(f32[264,128]{1,0:T(8,128)S(1)} %get-tuple-element.67), channel_id=1, source_target_pairs={{0,2},{1,3},{2,0},{3,1},{4,6},{5,7},{6,4},{7,5},{8,10},{9,11},{10,... | collective-permute-start | bytes 405512 | tf_op jit(solution)/shard_map/ppermute | solution.py:29
  91.3 7.2 %collective-permute-start.34 = (f32[264,128]{1,0:T(8,128)S(1)}, f32[264,128]{1,0:T(8,128)S(1)}, u32[]{:S(2)}, u32[]{:S(2)}) collective-permute-start(f32[264,128]{1,0:T(8,128)S(1)} %get-tuple-element.68), channel_id=1, source_target_pairs={{0,4},{1,5},{2,6},{3,7},{4,0},{5,1},{6,2},{7,3},{8,12},{9,13},{10,... | collective-permute-start | bytes 405512 | tf_op jit(solution)/shard_map/ppermute | solution.py:29
  93.1 7.0 %collective-permute-start.35 = (f32[264,128]{1,0:T(8,128)S(1)}, f32[264,128]{1,0:T(8,128)S(1)}, u32[]{:S(2)}, u32[]{:S(2)}) collective-permute-start(f32[264,128]{1,0:T(8,128)S(1)} %get-tuple-element.69), channel_id=1, source_target_pairs={{0,6},{1,7},{2,4},{3,5},{4,2},{5,3},{6,0},{7,1},{8,14},{9,15},{10,... | collective-permute-start | bytes 405512 | tf_op jit(solution)/shard_map/ppermute | solution.py:29
  (20 other events, 76.2 us)

commit v4 on v3

--- a/solution.py
+++ b/solution.py
@@ -42,7 +42,29 @@
     near = near_count(axis)
     if near > 1:
         part = merge_lse([part] + [swap(part, axis, d) for d in range(1, near)])
-    return [part] + [swap(part, axis, near * k) for k in range(1, 4)]
+    return merge_lse([part] + [swap(part, axis, near * k) for k in range(1, 4)])
+
+
+def exchange_both(both):
+    if near_count("tgt") != 2 or near_count("src") != 1:
+        whole = jnp.stack([exchange_lse(both[0], "tgt"), exchange_lse(both[1], "src")])
+        return whole, whole
+    odd = lax.rem(lax.axis_index("tgt"), 2) == 1
+    other = swap(both, "tgt", 1)
+    rows = merge_lse([both[0], other[0]])
+    part = jnp.where(odd, jnp.stack([rows, rows]), jnp.stack([both[1], other[1]]))
+    ntgt, nsrc = lax.axis_size("tgt"), lax.axis_size("src")
+
+    def swap_far(k):
+        pairs = [
+            (s * ntgt + t, s * ntgt + (t ^ (2 * k)) if t % 2 else (s ^ k) * ntgt + t)
+            for s in range(nsrc)
+            for t in range(ntgt)
+        ]
+        return lax.ppermute(part, ("src", "tgt"), pairs)
+
+    whole = merge_lse([part] + [swap_far(k) for k in range(1, 4)])
+    return whole, swap(whole, "tgt", 1)
 
 
 def gather_points(x_piece, y_piece, y_rows):
@@ -64,17 +86,11 @@
 
 def spread_near(found, axis):
     near = near_count(axis)
-    arrays = [array for _, _, array in found]
-    parts = [(mask, first, k, 0, array.shape[0]) for k, (mask, first, array) in enumerate(found)]
-    if near > 1:
-        whole = jnp.concatenate(arrays)
-        starts = [sum(a.shape[0] for a in arrays[:k]) for k in range(len(arrays))]
-        arrays = [whole] + [swap(whole, axis, d) for d in range(1, near)]
-        parts = [
-            (mask ^ d, first, d, start, count)
-            for d in range(near)
-            for (mask, first, _, _, count), start in zip(parts, starts)
-        ]
+    arrays, parts = [], []
+    for d in range(near):
+        for mask, first, array in found:
+            parts.append((mask ^ d, first, len(arrays), array.shape[0]))
+            arrays.append(swap(array, axis, d) if d else array)
     return arrays, parts
 
 
@@ -97,8 +113,9 @@
 
 def column_scores(stream_ref, q, split_ref, lane_ref, p):
     blocks = stream_ref.shape[1]
-    lane = lax.broadcasted_iota(jnp.int32, split_ref.shape, 1)
+    lane = lax.broadcasted_iota(jnp.int32, (16, LANES), 1)
     pick = jnp.where((lane < 3 * blocks) & (lax.rem(lane, blocks) == q), 1.0, 0.0).astype(jnp.bfloat16)
+    pick = jnp.concatenate([pick] * (split_ref.shape[0] // 16), axis=0)
     score = lax.dot_general(
         jnp.concatenate([whole_block(stream_ref, q), split_ref[...]], axis=1),
         jnp.concatenate([whole_block(lane_ref, p), pick], axis=1),
@@ -126,17 +143,17 @@
     return top[:, 0] + jnp.log2(jnp.maximum(total, 1.0))
 
 
-def visit_pairs(count_ref, list_ref, tb, group, work):
-    count = count_ref[0]
+def visit_pairs(list_ref, tb, group, work):
+    count = list_ref[0]
 
     @pl.loop(0, pl.cdiv(count, group))
     def _(step):
         places = [step * group + k for k in range(group)]
-        codes = [list_ref[place] for place in places]
+        codes = [list_ref[1 + place] for place in places]
         work([(code // tb, lax.rem(code, tb), place < count) for place, code in zip(places, codes)])
 
 
-def sweep(count_ref, list_ref, x_ref, y_ref, u, h, rows_ref, cols_ref, scratch):
+def sweep(list_ref, x_ref, y_ref, u, h, both_ref, scratch):
     u_split_ref, h_split_ref, rpeak_ref, rsum_ref, cpeak_ref, csum_ref = scratch
     sb, tb = x_ref.shape[1], y_ref.shape[1]
     split_columns(u, u_split_ref)
@@ -154,9 +171,9 @@
             rpeak_ref[pl.ds(p * tb + q, 1), :], rsum_ref[pl.ds(p * tb + q, 1), :] = row
             cpeak_ref[pl.ds(q * sb + p, 1), :], csum_ref[pl.ds(q * sb + p, 1), :] = col
 
-    visit_pairs(count_ref, list_ref, tb, GROUP, work)
-    rows_ref[...] = merge_slots(rpeak_ref, rsum_ref, sb)
-    cols_ref[...] = merge_slots(cpeak_ref, csum_ref, tb)
+    visit_pairs(list_ref, tb, GROUP, work)
+    both_ref[0] = merge_slots(rpeak_ref, rsum_ref, sb)
+    both_ref[1] = merge_slots(cpeak_ref, csum_ref, tb)
 
 
 def sweep_scratch(sb, tb, blk):
@@ -181,10 +198,9 @@
     ]
 
 
-def list_kernel(keep_ref, count_ref, list_ref):
+def list_kernel(keep_ref, list_ref):
     sb, tb = keep_ref.shape
-
-    n, last = jnp.int32(0), jnp.int32(0)
+    n, last = jnp.int32(1), jnp.int32(0)
     for code in range(sb * tb):
         kept = keep_ref[code // tb, code % tb] > 0
         list_ref[n] = code
@@ -192,21 +208,21 @@
         last = jnp.where(kept, code, last)
     for k in range(GROUP):
         list_ref[n + k] = last
-    count_ref[0] = n
+    list_ref[0] = n - 1
 
 
 def assemble(place, counts_ref, parts, part_refs, points_ref, vec_ref):
     n, blocks, piece, width = points_ref.shape
     blk = n * piece
     vec_ref[...] = jnp.zeros(vec_ref.shape, jnp.float32)
-    for mask, first, k, start, count in parts:
+    for mask, first, k, count in parts:
         owner = jnp.bitwise_xor(place, mask)
         rows = min(count, blocks * piece - first)
-        points_ref[owner, first // piece : (first + rows) // piece] = part_refs[k][start : start + rows].reshape(
+        points_ref[owner, first // piece : (first + rows) // piece] = part_refs[k][:rows].reshape(
             rows // piece, piece, width
         )
         if rows < count:
-            vecs = part_refs[k][start + rows : start + count].astype(jnp.float32)
+            vecs = part_refs[k][rows:count].astype(jnp.float32)
             tile = owner * piece // LANES
             vec_ref[0, tile] += vecs[:blocks]
             vec_ref[1, tile] += vecs[blocks:]
@@ -232,42 +248,51 @@
     return potential, half, base
 
 
-def first_kernel(x_parts, y_parts, src_counts_ref, tgt_counts_ref, count_ref, list_ref, *refs):
+def first_kernel(x_parts, y_parts, src_counts_ref, tgt_counts_ref, list_ref, *refs):
     nx = 1 + max(part[2] for part in x_parts)
     ny = 1 + max(part[2] for part in y_parts)
     x_in, y_in, refs = refs[:nx], refs[nx : nx + ny], refs[nx + ny :]
-    x_ref, y_ref, fixed_ref, f_ref, g_ref, rows_ref, cols_ref, xvec_ref, yvec_ref = refs[:9]
+    x_ref, y_ref, fixed_ref, f_ref, g_ref, both_ref, xvec_ref, yvec_ref = refs[:8]
     f, x_half, x_base = assemble(lax.axis_index("tgt"), src_counts_ref, x_parts, x_in, x_ref, xvec_ref)
     g, y_half, y_base = assemble(lax.axis_index("src"), tgt_counts_ref, y_parts, y_in, y_ref, yvec_ref)
     f_ref[...] = f
     g_ref[...] = g
     for k, vec in enumerate((x_half, x_base, y_half, y_base)):
         fixed_ref[k] = vec
-    sweep(count_ref, list_ref, x_ref, y_ref, f + x_base, g + y_base, rows_ref, cols_ref, refs[9:])
-
-
-def updated(old, half, part_refs):
-    return 0.5 * (old + (half - merge_lse([ref[...] for ref in part_refs])))
-
-
-def step_kernel(count_ref, list_ref, x_ref, y_ref, fixed_ref, f_in_ref, g_in_ref, *refs):
-    row_refs, col_refs, refs = refs[:4], refs[4:8], refs[8:]
-    f_ref, g_ref, rows_ref, cols_ref = refs[:4]
-    f = updated(f_in_ref[...], fixed_ref[0], row_refs)
-    g = updated(g_in_ref[...], fixed_ref[2], col_refs)
+    sweep(list_ref, x_ref, y_ref, f + x_base, g + y_base, both_ref, refs[8:])
+
+
+def chosen(whole_ref, other_ref, paired):
+    if not paired:
+        return whole_ref[0], whole_ref[1]
+    odd = lax.rem(lax.axis_index("tgt"), 2) == 1
+    return jnp.where(odd, whole_ref[0], other_ref[0]), jnp.where(odd, other_ref[1], whole_ref[0])
+
+
+def updated(f, g, fixed_ref, whole_ref, other_ref, paired):
+    rows, cols = chosen(whole_ref, other_ref, paired)
+    return 0.5 * (f + (fixed_ref[0] - rows)), 0.5 * (g + (fixed_ref[2] - cols))
+
+
+def step_kernel(paired, list_ref, x_ref, y_ref, fixed_ref, f_in_ref, g_in_ref, whole_ref, other_ref, *refs):
+    f_ref, g_ref, both_ref = refs[:3]
+    f, g = updated(f_in_ref[...], g_in_ref[...], fixed_ref, whole_ref, other_ref, paired)
     f_ref[...] = f
     g_ref[...] = g
-    sweep(count_ref, list_ref, x_ref, y_ref, f + fixed_ref[1], g + fixed_ref[3], rows_ref, cols_ref, refs[4:])
-
-
-def project_kernel(near, count_ref, list_ref, x_ref, y_ref, fixed_ref, g_in_ref, *refs):
-    col_refs, g_ref, out_refs = refs[:4], refs[4], refs[5 : 5 + near]
-    split_ref, turned_ref, peak_ref, sum_ref, acc_ref, image_ref = refs[5 + near :]
+    sweep(list_ref, x_ref, y_ref, f + fixed_ref[1], g + fixed_ref[3], both_ref, refs[3:])
+
+
+def project_kernel(
+    near, paired, list_ref, x_ref, y_ref, fixed_ref, f_in_ref, g_in_ref, whole_ref, other_ref, *refs
+):
+    f_ref, g_ref, out_refs = refs[0], refs[1], refs[2 : 2 + near]
+    split_ref, turned_ref, peak_ref, sum_ref, acc_ref, image_ref = refs[2 + near :]
     n, sb, piece, width = x_ref.shape
     tb = y_ref.shape[1]
     blk = n * piece
-    g = updated(g_in_ref[...], fixed_ref[2], col_refs)
-    g_ref[...] = g
+    f, g = updated(f_in_ref[...], g_in_ref[...], fixed_ref, whole_ref, other_ref, paired)
+    f_ref[...] = f * (1.0 / UNIT)
+    g_ref[...] = g * (1.0 / UNIT)
     split_columns(g + fixed_ref[3], split_ref)
     for q in range(tb):
         turned_ref[q] = whole_block(y_ref, q).T
@@ -294,7 +319,7 @@
             sum_ref[p] = sum_ref[p] * before + total * here
             acc_ref[p] = acc_ref[p] * before + moved * here
 
-    visit_pairs(count_ref, list_ref, tb, MOVE_GROUP, move)
+    visit_pairs(list_ref, tb, MOVE_GROUP, move)
     rows = []
     for p in range(sb):
         total = jnp.maximum(sum_ref[p], 1.0)
@@ -378,14 +403,12 @@
     sb, src_piece, width = src_points.shape
     tb, tgt_piece, _ = tgt_points.shape
     blk = src_piece * ntgt
-    count, pairs = pl.pallas_call(
+    pairs = pl.pallas_call(
         list_kernel,
-        out_shape=(
-            jax.ShapeDtypeStruct((1,), jnp.int32),
-            jax.ShapeDtypeStruct((sb * tb + GROUP,), jnp.int32),
-        ),
+        out_shape=jax.ShapeDtypeStruct((1 + sb * tb + GROUP,), jnp.int32),
         in_specs=[SMEM],
-        out_specs=(SMEM, SMEM),
+        out_specs=SMEM,
+        compiler_params=PARAMS,
         name="kept_pairs",
     )(keep)
 
@@ -402,8 +425,9 @@
     )(src_points, src_mass, src_potential, tgt_points, tgt_mass, tgt_potential)
     (x_in, x_parts), (y_in, y_parts) = gather_points(x_packed, y_packed, y_rows)
 
-    vectors = (f32(sb, blk), f32(tb, blk), f32(sb, blk), f32(tb, blk))
-    x, y, fixed, f, g, rows, cols = pl.pallas_call(
+    paired = near == 2 and near_count("src") == 1
+    vectors = (f32(sb, blk), f32(tb, blk), f32(2, sb, blk))
+    x, y, fixed, f, g, both = pl.pallas_call(
         functools.partial(first_kernel, x_parts, y_parts),
         out_shape=(
             jax.ShapeDtypeStruct((ntgt, sb, src_piece, width), jnp.bfloat16),
@@ -411,8 +435,8 @@
             f32(4, sb, blk),
         )
         + vectors,
-        in_specs=[SMEM] * 4 + [VMEM] * (len(x_in) + len(y_in)),
-        out_specs=(VMEM,) * 7,
+        in_specs=[SMEM] * 3 + [VMEM] * (len(x_in) + len(y_in)),
+        out_specs=(VMEM,) * 6,
         scratch_shapes=[
             pltpu.VMEM((2, blk // LANES, sb, LANES), jnp.float32),
             pltpu.VMEM((2, blk // LANES, tb, LANES), jnp.float32),
@@ -420,34 +444,29 @@
         + sweep_scratch(sb, tb, blk),
         compiler_params=PARAMS,
         name="first_sweep",
-    )(src_counts, tgt_counts, count, pairs, *x_in, *y_in)
+    )(src_counts, tgt_counts, pairs, *x_in, *y_in)
 
     step = pl.pallas_call(
-        step_kernel,
+        functools.partial(step_kernel, paired),
         out_shape=vectors,
-        in_specs=[SMEM] * 2 + [VMEM] * 13,
-        out_specs=(VMEM,) * 4,
+        in_specs=[SMEM] + [VMEM] * 7,
+        out_specs=(VMEM,) * 3,
         scratch_shapes=sweep_scratch(sb, tb, blk),
         compiler_params=PARAMS,
         name="sweep",
     )
     for _ in range(ITERS - 1):
-        row_parts = exchange_lse(rows, "tgt")
-        col_parts = exchange_lse(cols, "src")
-        f, g, rows, cols = step(count, pairs, x, y, fixed, f, g, *row_parts, *col_parts)
-
-    col_parts = exchange_lse(cols, "src")
-    row_parts = exchange_lse(rows, "tgt")
+        f, g, both = step(pairs, x, y, fixed, f, g, *exchange_both(both))
     tile = sb * src_piece + sb
-    g, *near_parts = pl.pallas_call(
-        functools.partial(project_kernel, near),
-        out_shape=(f32(tb, blk),) + (f32(4, tile, width),) * near,
-        in_specs=[SMEM] * 2 + [VMEM] * 8,
-        out_specs=(VMEM,) * (1 + near),
+    f, g, *near_parts = pl.pallas_call(
+        functools.partial(project_kernel, near, paired),
+        out_shape=(f32(sb, blk), f32(tb, blk)) + (f32(4, tile, width),) * near,
+        in_specs=[SMEM] + [VMEM] * 7,
+        out_specs=(VMEM,) * (2 + near),
         scratch_shapes=project_scratch(sb, tb, blk, width),
         compiler_params=PARAMS,
         name="project",
-    )(count, pairs, x, y, fixed, g, *col_parts)
+    )(pairs, x, y, fixed, f, g, *exchange_both(both))
     if near > 1:
         near_parts = near_parts[:1] + [swap(near_parts[d], "tgt", d) for d in range(1, near)]
     far_parts = pl.pallas_call(
@@ -470,9 +489,8 @@
         name="merge_far",
     )(*far_parts)
 
-    f = 0.5 * (f + (fixed[0] - merge_lse(row_parts)))
-    src_final = lax.dynamic_slice_in_dim(f * (1.0 / UNIT), lax.axis_index("tgt") * src_piece, src_piece, 1)
-    tgt_final = lax.dynamic_slice_in_dim(g * (1.0 / UNIT), lax.axis_index("src") * tgt_piece, tgt_piece, 1)
+    src_final = lax.dynamic_slice_in_dim(f, lax.axis_index("tgt") * src_piece, src_piece, 1)
+    tgt_final = lax.dynamic_slice_in_dim(g, lax.axis_index("src") * tgt_piece, tgt_piece, 1)
     return images, src_final, tgt_final
 
 

time: 102 us -> 96.2 us (0.943)
  starting transfers between devices: 46.7 us -> 29.8 us
  waiting for transfers between devices: 24.2 us -> 33.9 us
  Pallas kernels: 26.3 us -> 29.7 us
  other arithmetic: 1.44 us -> 0.24 us
    ppermute x40 -> x23, starting transfers between devices: 46.7 us -> 15.5 us  [swap(): lax.ppermute(part, axis, [(i, i ^ mask) for i in range(lax.axis_size(axis...]
    ppermute x0 -> x12, starting transfers between devices: none -> 14.3 us  [swap_far(): return lax.ppermute(part, ('src', 'tgt'), pairs)]
    ppermute x0 -> x12, waiting for transfers between devices: none -> 12.2 us  [swap_far(): return lax.ppermute(part, ('src', 'tgt'), pairs)]
    pallas_call x5, Pallas kernels: 18.3 us -> 21 us  [the longest x3 13.6 us: on_device(): f, g, both = step(pairs, x, y, fixed, f, g, *exchange_both(both))]
    ppermute x40 -> x23, waiting for transfers between devices: 24.2 us -> 21.7 us  [swap(): lax.ppermute(part, axis, [(i, i ^ mask) for i in range(lax.axis_size(axis...]
    unnamed x11 -> x10, local copies, waits for them, and re-layouts: 1.62 us -> 0.03 us
    mul x2 -> x0, other arithmetic: 1.35 us -> none  [the longest x1 0.68 us: on_device(): f * (1.0 / UNIT)]
    dynamic_slice x0 -> x2, local copies, waits for them, and re-layouts: none -> 1.33 us  [the longest x1 0.66 us: on_device(): lax.dynamic_slice_in_dim(f, lax.axis_index('tgt') * src_piece, src_piece, 1)]
  transfers between devices with their start and end apart: 40 -> 35, of which waited for: 21 -> 27; matrix products, arithmetic and copies ran while one was open for 2% -> 1% of each run, Pallas kernels for 7% -> 1%
where the time goes in v4:
time: 96.2 us; the launch traced here: 96 us
  waiting for transfers between devices  33.9 us (35%)
  starting transfers between devices  29.8 us (31%)
  Pallas kernels  29.7 us (31%)
  local copies, waits for them, and re-layouts  1.37 us (1%)
  between operations  0.97 us (1%)
    ppermute x23, waiting for transfers between devices, swap(): lax.ppermute(part, axis, [(i, i ^ mask) for i in range(lax.axis_size(axis...  21.7 us
    ppermute x23, starting transfers between devices, swap(): lax.ppermute(part, axis, [(i, i ^ mask) for i in range(lax.axis_size(axis...  15.5 us
    ppermute x12, starting transfers between devices, swap_far(): return lax.ppermute(part, ('src', 'tgt'), pairs)  14.3 us
    pallas_call x3, Pallas kernels, on_device(): f, g, both = step(pairs, x, y, fixed, f, g, *exchange_both(both))  13.6 us
    ppermute x12, waiting for transfers between devices, swap_far(): return lax.ppermute(part, ('src', 'tgt'), pairs)  12.2 us
    pallas_call x1, Pallas kernels, on_device(): pl.pallas_call(functools.partial(project_kernel, near, paired), out_shape...  5.98 us
    pallas_call x1, Pallas kernels, on_device(): pl.pallas_call(functools.partial(first_kernel, x_parts, y_parts), out_sha...  5.29 us
  transfers between devices with their start and end apart: 35, of which 27 were waited for; matrix products, arithmetic and copies ran while one was open for 1% of the time, Pallas kernels for 1%

profile of v4, /device:TPU:0, one launch (start us, length us, event | category | flops | bytes accessed | tf_op | source)
XLA Modules:
  0.0 96.0 jit_solution(13442434644737520692)
XLA Ops:
  0.6 1.7 %pack.1 = (bf16[272,128]{1,0:T(8,128)(2,1)}, bf16[528,128]{1,0:T(8,128)(2,1)}) custom-call(bf16[8,32,128]{2,1,0:T(8,128)(2,1)} %refs_0_.1, bf16[8,32]{1,0:T(8,128)(2,1)} %refs_1_.1, bf16[8,32]{1,0:T(8,128)(2,1)} %refs_2_.1, bf16[8,64,128]{2,1,0:T(8,128)(2,1)} %refs_3_.1, bf16[8,64]{1,0:T(8,128)(2,1)} %refs_4_.1, bf16[8,64]{1,0:T(8,128)(2,1)} %refs_5_.1), custom_call_target="tpu_custom_call" | custom-call | tf_op jit(solution)/shard_map/pack/pallas_call | solution.py:416
  2.4 5.0 %collective-permute-start.1 = (bf16[528,128]{1,0:T(8,128)(2,1)}, bf16[528,128]{1,0:T(8,128)(2,1)S(1)}, u32[]{:S(2)}, u32[]{:S(2)}) collective-permute-start(bf16[528,128]{1,0:T(8,128)(2,1)} %get-tuple-element.34.refs_8_), channel_id=1, source_target_pairs={{0,24},{8,16},{16,8},{24,0},{1,25},{9,17},{17,9},{25,1},{2,26},{10... | collective-permute-start | bytes 405512 | tf_op jit(solution)/shard_map/ppermute | solution.py:29
  7.4 2.4 %collective-permute-start.4 = (bf16[272,128]{1,0:T(8,128)(2,1)}, bf16[272,128]{1,0:T(8,128)(2,1)S(1)}, u32[]{:S(2)}, u32[]{:S(2)}) collective-permute-start(bf16[272,128]{1,0:T(8,128)(2,1)} %get-tuple-element.33.refs_0_), channel_id=1, source_target_pairs={{0,6},{1,7},{2,4},{3,5},{4,2},{5,3},{6,0},{7,1},{8,14},{9,15},{10,... | collective-permute-start | bytes 208904 | tf_op jit(solution)/shard_map/ppermute | solution.py:29
  10.9 2.0 %collective-permute-done.4.refs_3_ = bf16[272,128]{1,0:T(8,128)(2,1)S(1)} collective-permute-done((bf16[272,128]{1,0:T(8,128)(2,1)}, bf16[272,128]{1,0:T(8,128)(2,1)S(1)}, u32[]{:S(2)}, u32[]{:S(2)}) %collective-permute-start.4) | collective-permute-done | bytes 69664 | tf_op jit(solution)/shard_map/ppermute | solution.py:29
  13.0 1.4 %collective-permute-done.3.refs_2_ = bf16[272,128]{1,0:T(8,128)(2,1)S(1)} collective-permute-done((bf16[272,128]{1,0:T(8,128)(2,1)}, bf16[272,128]{1,0:T(8,128)(2,1)S(1)}, u32[]{:S(2)}, u32[]{:S(2)}) %collective-permute-start.3) | collective-permute-done | bytes 69664 | tf_op jit(solution)/shard_map/ppermute | solution.py:29
  16.6 1.2 %collective-permute-start.9 = (bf16[256,128]{1,0:T(8,128)(2,1)S(1)}, bf16[256,128]{1,0:T(8,128)(2,1)S(1)}, u32[]{:S(2)}, u32[]{:S(2)}) collective-permute-start(bf16[256,128]{1,0:T(8,128)(2,1)S(1)} %slice.54), channel_id=1, source_target_pairs={{0,8},{8,0},{16,24},{24,16},{1,9},{9,1},{17,25},{25,17},{2,10},{10... | collective-permute-start | bytes 196616 | tf_op jit(solution)/shard_map/ppermute | solution.py:29
  17.8 1.4 %kept_pairs.1.list_ref = s32[73]{0:T(128)S(1)} custom-call(s32[8,8]{1,0:T(8,128)S(1)} %copy-done.2), custom_call_target="tpu_custom_call" | custom-call | tf_op jit(solution)/shard_map/kept_pairs/pallas_call | solution.py:406
  19.2 2.7 %collective-permute-done.9.refs_11_ = bf16[256,128]{1,0:T(8,128)(2,1)S(1)} collective-permute-done((bf16[256,128]{1,0:T(8,128)(2,1)S(1)}, bf16[256,128]{1,0:T(8,128)(2,1)S(1)}, u32[]{:S(2)}, u32[]{:S(2)}) %collective-permute-start.9) | collective-permute-done | bytes 65568 | tf_op jit(solution)/shard_map/ppermute | solution.py:29
  21.9 5.3 %first_sweep.1 = (bf16[8,8,32,128]{3,2,1,0:T(8,128)(2,1)S(1)}, bf16[4,8,64,128]{3,2,1,0:T(8,128)(2,1)S(1)}, f32[4,8,256]{2,1,0:T(8,128)S(1)}, f32[8,256]{1,0:T(8...) custom-call(s32[8]{0:T(128)S(1)} %copy-done.3, s32[8]{0:T(128)S(1)} %copy-done.4, s32[73]{0:T(128)S(1)} %kept_pairs.1.list_ref, ...), custom_call_target="tpu_custom_call" | custom-call | tf_op jit(solution)/shard_map/first_sweep/pallas_call | solution.py:430
  28.6 2.0 %collective-permute-start.14 = (f32[2,8,256]{2,1,0:T(8,128)S(1)}, f32[2,8,256]{2,1,0:T(8,128)S(1)}, u32[]{:S(2)}, u32[]{:S(2)}) collective-permute-start(f32[2,8,256]{2,1,0:T(8,128)S(1)} %maximum_select_fusion), channel_id=1, source_target_pairs={{0,24},{1,7},{2,26},{3,5},{4,28},{5,3},{6,30},{7,1},{8,16},{9,15},... | collective-permute-start | bytes 49160 | tf_op jit(solution)/shard_map/ppermute | solution.py:64
  30.6 1.5 %collective-permute-start.12 = (f32[2,8,256]{2,1,0:T(8,128)S(1)}, f32[2,8,256]{2,1,0:T(8,128)S(1)}, u32[]{:S(2)}, u32[]{:S(2)}) collective-permute-start(f32[2,8,256]{2,1,0:T(8,128)S(1)} %maximum_select_fusion), channel_id=1, source_target_pairs={{0,8},{1,3},{2,10},{3,1},{4,12},{5,7},{6,14},{7,5},{8,0},{9,11},{1... | collective-permute-start | bytes 49160 | tf_op jit(solution)/shard_map/ppermute | solution.py:64
  35.7 4.5 %sweep.3 = (f32[8,256]{1,0:T(8,128)S(1)}, f32[8,256]{1,0:T(8,128)S(1)}, f32[2,8,256]{2,1,0:T(8,128)S(1)}) custom-call(s32[73]{0:T(128)S(1)} %kept_pairs.1.list_ref, bf16[8,8,32,128]{3,2,1,0:T(8,128)(2,1)S(1)} %get-tuple-element.40.x_ref, bf16[4,8,64,128]{3,2,1,0:T(8,128)(2,1)S(1)} %get-tuple-element.41.y_ref, f32[4,8,256]{2,1,0:T(8,128)S(1)} %get-tuple-element.42.fixed_ref, ...), custom_call_target="tpu_custom_call" | custom-call | tf_op jit(solution)/shard_map/sweep/pallas_call | solution.py:459
  41.6 3.6 %collective-permute-start.19 = (f32[2,8,256]{2,1,0:T(8,128)S(1)}, f32[2,8,256]{2,1,0:T(8,128)S(1)}, u32[]{:S(2)}, u32[]{:S(2)}) collective-permute-start(f32[2,8,256]{2,1,0:T(8,128)S(1)} %maximum_select_fusion.1), channel_id=1, source_target_pairs={{0,24},{1,7},{2,26},{3,5},{4,28},{5,3},{6,30},{7,1},{8,16},{9,15},... | collective-permute-start | bytes 49160 | tf_op jit(solution)/shard_map/ppermute | solution.py:64
  47.2 1.7 %collective-permute-done.17 = f32[2,8,256]{2,1,0:T(8,128)S(1)} collective-permute-done((f32[2,8,256]{2,1,0:T(8,128)S(1)}, f32[2,8,256]{2,1,0:T(8,128)S(1)}, u32[]{:S(2)}, u32[]{:S(2)}) %collective-permute-start.17) | collective-permute-done | bytes 16416 | tf_op jit(solution)/shard_map/ppermute | solution.py:64
  50.2 4.6 %sweep.4 = (f32[8,256]{1,0:T(8,128)S(1)}, f32[8,256]{1,0:T(8,128)S(1)}, f32[2,8,256]{2,1,0:T(8,128)S(1)}) custom-call(s32[73]{0:T(128)S(1)} %kept_pairs.1.list_ref, bf16[8,8,32,128]{3,2,1,0:T(8,128)(2,1)S(1)} %get-tuple-element.40.x_ref, bf16[4,8,64,128]{3,2,1,0:T(8,128)(2,1)S(1)} %get-tuple-element.41.y_ref, f32[4,8,256]{2,1,0:T(8,128)S(1)} %get-tuple-element.42.fixed_ref, ...), custom_call_target="tpu_custom_call" | custom-call | tf_op jit(solution)/shard_map/sweep/pallas_call | solution.py:459
  56.1 2.3 %collective-permute-start.24 = (f32[2,8,256]{2,1,0:T(8,128)S(1)}, f32[2,8,256]{2,1,0:T(8,128)S(1)}, u32[]{:S(2)}, u32[]{:S(2)}) collective-permute-start(f32[2,8,256]{2,1,0:T(8,128)S(1)} %maximum_select_fusion.2), channel_id=1, source_target_pairs={{0,24},{1,7},{2,26},{3,5},{4,28},{5,3},{6,30},{7,1},{8,16},{9,15},... | collective-permute-start | bytes 49160 | tf_op jit(solution)/shard_map/ppermute | solution.py:64
  63.4 4.6 %sweep.5 = (f32[8,256]{1,0:T(8,128)S(1)}, f32[8,256]{1,0:T(8,128)S(1)}, f32[2,8,256]{2,1,0:T(8,128)S(1)}) custom-call(s32[73]{0:T(128)S(1)} %kept_pairs.1.list_ref, bf16[8,8,32,128]{3,2,1,0:T(8,128)(2,1)S(1)} %get-tuple-element.40.x_ref, bf16[4,8,64,128]{3,2,1,0:T(8,128)(2,1)S(1)} %get-tuple-element.41.y_ref, f32[4,8,256]{2,1,0:T(8,128)S(1)} %get-tuple-element.42.fixed_ref, ...), custom_call_target="tpu_custom_call" | custom-call | tf_op jit(solution)/shard_map/sweep/pallas_call | solution.py:459
  69.3 3.3 %collective-permute-start.29 = (f32[2,8,256]{2,1,0:T(8,128)S(1)}, f32[2,8,256]{2,1,0:T(8,128)S(1)}, u32[]{:S(2)}, u32[]{:S(2)}) collective-permute-start(f32[2,8,256]{2,1,0:T(8,128)S(1)} %maximum_select_fusion.3), channel_id=1, source_target_pairs={{0,24},{1,7},{2,26},{3,5},{4,28},{5,3},{6,30},{7,1},{8,16},{9,15},... | collective-permute-start | bytes 49160 | tf_op jit(solution)/shard_map/ppermute | solution.py:64
  74.9 1.4 %collective-permute-done.27 = f32[2,8,256]{2,1,0:T(8,128)S(1)} collective-permute-done((f32[2,8,256]{2,1,0:T(8,128)S(1)}, f32[2,8,256]{2,1,0:T(8,128)S(1)}, u32[]{:S(2)}, u32[]{:S(2)}) %collective-permute-start.27) | collective-permute-done | bytes 16416 | tf_op jit(solution)/shard_map/ppermute | solution.py:64
  77.7 6.0 %project.1 = (f32[8,256]{1,0:T(8,128)S(1)}, f32[8,256]{1,0:T(8,128)S(1)}, f32[4,264,128]{2,1,0:T(8,128)S(1)}, f32[4,264,128]{2,1,0:T(8,128)S(1)}) custom-call(s32[73]{0:T(128)S(1)} %kept_pairs.1.list_ref, bf16[8,8,32,128]{3,2,1,0:T(8,128)(2,1)S(1)} %get-tuple-element.40.x_ref, bf16[4,8,64,128]{3,2,1,0:T(8,128)(2,1)S(1)} %get-tuple-element.41.y_ref, ...), custom_call_target="tpu_custom_call" | custom-call | tf_op jit(solution)/shard_map/project/pallas_call | solution.py:461
  83.7 1.9 %collective-permute-done.31.refs_1_ = f32[4,264,128]{2,1,0:T(8,128)S(1)} collective-permute-done((f32[4,264,128]{2,1,0:T(8,128)S(1)}, f32[4,264,128]{2,1,0:T(8,128)S(1)}, u32[]{:S(2)}, u32[]{:S(2)}) %collective-permute-start.31) | collective-permute-done | bytes 540704 | tf_op jit(solution)/shard_map/ppermute | solution.py:29
  86.4 3.4 %collective-permute-start.34 = (f32[264,128]{1,0:T(8,128)S(1)}, f32[264,128]{1,0:T(8,128)S(1)}, u32[]{:S(2)}, u32[]{:S(2)}) collective-permute-start(f32[264,128]{1,0:T(8,128)S(1)} %get-tuple-element.60), channel_id=1, source_target_pairs={{0,6},{1,7},{2,4},{3,5},{4,2},{5,3},{6,0},{7,1},{8,14},{9,15},{10,... | collective-permute-start | bytes 405512 | tf_op jit(solution)/shard_map/ppermute | solution.py:29
  91.2 1.6 %collective-permute-done.32.refs_1_ = f32[264,128]{1,0:T(8,128)S(1)} collective-permute-done((f32[264,128]{1,0:T(8,128)S(1)}, f32[264,128]{1,0:T(8,128)S(1)}, u32[]{:S(2)}, u32[]{:S(2)}) %collective-permute-start.32) | collective-permute-done | bytes 135200 | tf_op jit(solution)/shard_map/ppermute | solution.py:29
  92.8 2.2 %collective-permute-done.33.refs_2_ = f32[264,128]{1,0:T(8,128)S(1)} collective-permute-done((f32[264,128]{1,0:T(8,128)S(1)}, f32[264,128]{1,0:T(8,128)S(1)}, u32[]{:S(2)}, u32[]{:S(2)}) %collective-permute-start.33) | collective-permute-done | bytes 135200 | tf_op jit(solution)/shard_map/ppermute | solution.py:29
  (81 shorter events, 27.2 us)
Async XLA Ops:
  2.4 12.5 %collective-permute-start.1 = (bf16[528,128]{1,0:T(8,128)(2,1)}, bf16[528,128]{1,0:T(8,128)(2,1)S(1)}, u32[]{:S(2)}, u32[]{:S(2)}) collective-permute-start(bf16[528,128]{1,0:T(8,128)(2,1)} %get-tuple-element.34.refs_8_), channel_id=1, source_target_pairs={{0,24},{8,16},{16,8},{24,0},{1,25},{9,17},{17,9},{25,1},{2,26},{10... | collective-permute-start | bytes 405512 | tf_op jit(solution)/shard_map/ppermute | solution.py:29
  7.4 7.5 %collective-permute-start = (bf16[528,128]{1,0:T(8,128)(2,1)}, bf16[528,128]{1,0:T(8,128)(2,1)S(1)}, u32[]{:S(2)}, u32[]{:S(2)}) collective-permute-start(bf16[528,128]{1,0:T(8,128)(2,1)} %get-tuple-element.34.refs_8_), channel_id=1, source_target_pairs={{0,8},{8,0},{16,24},{24,16},{1,9},{9,1},{17,25},{25,17},{2,10},{10... | collective-permute-start | bytes 405512 | tf_op jit(solution)/shard_map/ppermute | solution.py:29
  7.4 5.5 %collective-permute-start.4 = (bf16[272,128]{1,0:T(8,128)(2,1)}, bf16[272,128]{1,0:T(8,128)(2,1)S(1)}, u32[]{:S(2)}, u32[]{:S(2)}) collective-permute-start(bf16[272,128]{1,0:T(8,128)(2,1)} %get-tuple-element.33.refs_0_), channel_id=1, source_target_pairs={{0,6},{1,7},{2,4},{3,5},{4,2},{5,3},{6,0},{7,1},{8,14},{9,15},{10,... | collective-permute-start | bytes 208904 | tf_op jit(solution)/shard_map/ppermute | solution.py:29
  9.9 4.5 %collective-permute-start.3 = (bf16[272,128]{1,0:T(8,128)(2,1)}, bf16[272,128]{1,0:T(8,128)(2,1)S(1)}, u32[]{:S(2)}, u32[]{:S(2)}) collective-permute-start(bf16[272,128]{1,0:T(8,128)(2,1)} %get-tuple-element.33.refs_0_), channel_id=1, source_target_pairs={{0,4},{1,5},{2,6},{3,7},{4,0},{5,1},{6,2},{7,3},{8,12},{9,13},{10,... | collective-permute-start | bytes 208904 | tf_op jit(solution)/shard_map/ppermute | solution.py:29
  10.4 4.5 %collective-permute-start.2 = (bf16[272,128]{1,0:T(8,128)(2,1)}, bf16[272,128]{1,0:T(8,128)(2,1)S(1)}, u32[]{:S(2)}, u32[]{:S(2)}) collective-permute-start(bf16[272,128]{1,0:T(8,128)(2,1)} %get-tuple-element.33.refs_0_), channel_id=1, source_target_pairs={{0,2},{1,3},{2,0},{3,1},{4,6},{5,7},{6,4},{7,5},{8,10},{9,11},{10,... | collective-permute-start | bytes 208904 | tf_op jit(solution)/shard_map/ppermute | solution.py:29
  14.9 6.9 %collective-permute-start.10 = (bf16[272,128]{1,0:T(8,128)(2,1)S(1)}, bf16[272,128]{1,0:T(8,128)(2,1)S(1)}, u32[]{:S(2)}, u32[]{:S(2)}) collective-permute-start(bf16[272,128]{1,0:T(8,128)(2,1)S(1)} %slice.55), channel_id=1, source_target_pairs={{0,24},{8,16},{16,8},{24,0},{1,25},{9,17},{17,9},{25,1},{2,26},{10... | collective-permute-start | bytes 208904 | tf_op jit(solution)/shard_map/ppermute | solution.py:29
  16.0 5.9 %collective-permute-start.6 = (bf16[272,128]{1,0:T(8,128)(2,1)S(1)}, bf16[272,128]{1,0:T(8,128)(2,1)S(1)}, u32[]{:S(2)}, u32[]{:S(2)}) collective-permute-start(bf16[272,128]{1,0:T(8,128)(2,1)S(1)} %collective-permute-done.2.refs_1_), channel_id=1, source_target_pairs={{0,1},{1,0},{2,3},{3,2},{4,5},{5,4},{6,7},{7,6},{8,9},{9,8},{10,11... | collective-permute-start | bytes 208904 | tf_op jit(solution)/shard_map/ppermute | solution.py:29
  16.0 5.9 %collective-permute-start.7 = (bf16[272,128]{1,0:T(8,128)(2,1)S(1)}, bf16[272,128]{1,0:T(8,128)(2,1)S(1)}, u32[]{:S(2)}, u32[]{:S(2)}) collective-permute-start(bf16[272,128]{1,0:T(8,128)(2,1)S(1)} %collective-permute-done.3.refs_2_), channel_id=1, source_target_pairs={{0,1},{1,0},{2,3},{3,2},{4,5},{5,4},{6,7},{7,6},{8,9},{9,8},{10,11... | collective-permute-start | bytes 208904 | tf_op jit(solution)/shard_map/ppermute | solution.py:29
  16.5 5.4 %collective-permute-start.8 = (bf16[272,128]{1,0:T(8,128)(2,1)S(1)}, bf16[272,128]{1,0:T(8,128)(2,1)S(1)}, u32[]{:S(2)}, u32[]{:S(2)}) collective-permute-start(bf16[272,128]{1,0:T(8,128)(2,1)S(1)} %collective-permute-done.4.refs_3_), channel_id=1, source_target_pairs={{0,1},{1,0},{2,3},{3,2},{4,5},{5,4},{6,7},{7,6},{8,9},{9,8},{10,11... | collective-permute-start | bytes 208904 | tf_op jit(solution)/shard_map/ppermute | solution.py:29
  16.6 5.3 %collective-permute-start.9 = (bf16[256,128]{1,0:T(8,128)(2,1)S(1)}, bf16[256,128]{1,0:T(8,128)(2,1)S(1)}, u32[]{:S(2)}, u32[]{:S(2)}) collective-permute-start(bf16[256,128]{1,0:T(8,128)(2,1)S(1)} %slice.54), channel_id=1, source_target_pairs={{0,8},{8,0},{16,24},{24,16},{1,9},{9,1},{17,25},{25,17},{2,10},{10... | collective-permute-start | bytes 196616 | tf_op jit(solution)/shard_map/ppermute | solution.py:29
  28.5 4.7 %collective-permute-start.13 = (f32[2,8,256]{2,1,0:T(8,128)S(1)}, f32[2,8,256]{2,1,0:T(8,128)S(1)}, u32[]{:S(2)}, u32[]{:S(2)}) collective-permute-start(f32[2,8,256]{2,1,0:T(8,128)S(1)} %maximum_select_fusion), channel_id=1, source_target_pairs={{0,16},{1,5},{2,18},{3,7},{4,20},{5,1},{6,22},{7,3},{8,24},{9,13},... | collective-permute-start | bytes 49160 | tf_op jit(solution)/shard_map/ppermute | solution.py:64
  28.6 5.6 %collective-permute-start.14 = (f32[2,8,256]{2,1,0:T(8,128)S(1)}, f32[2,8,256]{2,1,0:T(8,128)S(1)}, u32[]{:S(2)}, u32[]{:S(2)}) collective-permute-start(f32[2,8,256]{2,1,0:T(8,128)S(1)} %maximum_select_fusion), channel_id=1, source_target_pairs={{0,24},{1,7},{2,26},{3,5},{4,28},{5,3},{6,30},{7,1},{8,16},{9,15},... | collective-permute-start | bytes 49160 | tf_op jit(solution)/shard_map/ppermute | solution.py:64
  30.6 3.8 %collective-permute-start.12 = (f32[2,8,256]{2,1,0:T(8,128)S(1)}, f32[2,8,256]{2,1,0:T(8,128)S(1)}, u32[]{:S(2)}, u32[]{:S(2)}) collective-permute-start(f32[2,8,256]{2,1,0:T(8,128)S(1)} %maximum_select_fusion), channel_id=1, source_target_pairs={{0,8},{1,3},{2,10},{3,1},{4,12},{5,7},{6,14},{7,5},{8,0},{9,11},{1... | collective-permute-start | bytes 49160 | tf_op jit(solution)/shard_map/ppermute | solution.py:64
  41.5 4.7 %collective-permute-start.18 = (f32[2,8,256]{2,1,0:T(8,128)S(1)}, f32[2,8,256]{2,1,0:T(8,128)S(1)}, u32[]{:S(2)}, u32[]{:S(2)}) collective-permute-start(f32[2,8,256]{2,1,0:T(8,128)S(1)} %maximum_select_fusion.1), channel_id=1, source_target_pairs={{0,16},{1,5},{2,18},{3,7},{4,20},{5,1},{6,22},{7,3},{8,24},{9,13},... | collective-permute-start | bytes 49160 | tf_op jit(solution)/shard_map/ppermute | solution.py:64
  41.6 5.6 %collective-permute-start.19 = (f32[2,8,256]{2,1,0:T(8,128)S(1)}, f32[2,8,256]{2,1,0:T(8,128)S(1)}, u32[]{:S(2)}, u32[]{:S(2)}) collective-permute-start(f32[2,8,256]{2,1,0:T(8,128)S(1)} %maximum_select_fusion.1), channel_id=1, source_target_pairs={{0,24},{1,7},{2,26},{3,5},{4,28},{5,3},{6,30},{7,1},{8,16},{9,15},... | collective-permute-start | bytes 49160 | tf_op jit(solution)/shard_map/ppermute | solution.py:64
  45.1 3.7 %collective-permute-start.17 = (f32[2,8,256]{2,1,0:T(8,128)S(1)}, f32[2,8,256]{2,1,0:T(8,128)S(1)}, u32[]{:S(2)}, u32[]{:S(2)}) collective-permute-start(f32[2,8,256]{2,1,0:T(8,128)S(1)} %maximum_select_fusion.1), channel_id=1, source_target_pairs={{0,8},{1,3},{2,10},{3,1},{4,12},{5,7},{6,14},{7,5},{8,0},{9,11},{1... | collective-permute-start | bytes 49160 | tf_op jit(solution)/shard_map/ppermute | solution.py:64
  56.0 4.7 %collective-permute-start.23 = (f32[2,8,256]{2,1,0:T(8,128)S(1)}, f32[2,8,256]{2,1,0:T(8,128)S(1)}, u32[]{:S(2)}, u32[]{:S(2)}) collective-permute-start(f32[2,8,256]{2,1,0:T(8,128)S(1)} %maximum_select_fusion.2), channel_id=1, source_target_pairs={{0,16},{1,5},{2,18},{3,7},{4,20},{5,1},{6,22},{7,3},{8,24},{9,13},... | collective-permute-start | bytes 49160 | tf_op jit(solution)/shard_map/ppermute | solution.py:64
  56.1 5.6 %collective-permute-start.24 = (f32[2,8,256]{2,1,0:T(8,128)S(1)}, f32[2,8,256]{2,1,0:T(8,128)S(1)}, u32[]{:S(2)}, u32[]{:S(2)}) collective-permute-start(f32[2,8,256]{2,1,0:T(8,128)S(1)} %maximum_select_fusion.2), channel_id=1, source_target_pairs={{0,24},{1,7},{2,26},{3,5},{4,28},{5,3},{6,30},{7,1},{8,16},{9,15},... | collective-permute-start | bytes 49160 | tf_op jit(solution)/shard_map/ppermute | solution.py:64
  58.4 3.7 %collective-permute-start.22 = (f32[2,8,256]{2,1,0:T(8,128)S(1)}, f32[2,8,256]{2,1,0:T(8,128)S(1)}, u32[]{:S(2)}, u32[]{:S(2)}) collective-permute-start(f32[2,8,256]{2,1,0:T(8,128)S(1)} %maximum_select_fusion.2), channel_id=1, source_target_pairs={{0,8},{1,3},{2,10},{3,1},{4,12},{5,7},{6,14},{7,5},{8,0},{9,11},{1... | collective-permute-start | bytes 49160 | tf_op jit(solution)/shard_map/ppermute | solution.py:64
  69.2 4.7 %collective-permute-start.28 = (f32[2,8,256]{2,1,0:T(8,128)S(1)}, f32[2,8,256]{2,1,0:T(8,128)S(1)}, u32[]{:S(2)}, u32[]{:S(2)}) collective-permute-start(f32[2,8,256]{2,1,0:T(8,128)S(1)} %maximum_select_fusion.3), channel_id=1, source_target_pairs={{0,16},{1,5},{2,18},{3,7},{4,20},{5,1},{6,22},{7,3},{8,24},{9,13},... | collective-permute-start | bytes 49160 | tf_op jit(solution)/shard_map/ppermute | solution.py:64
  69.3 5.6 %collective-permute-start.29 = (f32[2,8,256]{2,1,0:T(8,128)S(1)}, f32[2,8,256]{2,1,0:T(8,128)S(1)}, u32[]{:S(2)}, u32[]{:S(2)}) collective-permute-start(f32[2,8,256]{2,1,0:T(8,128)S(1)} %maximum_select_fusion.3), channel_id=1, source_target_pairs={{0,24},{1,7},{2,26},{3,5},{4,28},{5,3},{6,30},{7,1},{8,16},{9,15},... | collective-permute-start | bytes 49160 | tf_op jit(solution)/shard_map/ppermute | solution.py:64
  86.3 6.5 %collective-permute-start.32 = (f32[264,128]{1,0:T(8,128)S(1)}, f32[264,128]{1,0:T(8,128)S(1)}, u32[]{:S(2)}, u32[]{:S(2)}) collective-permute-start(f32[264,128]{1,0:T(8,128)S(1)} %get-tuple-element.58), channel_id=1, source_target_pairs={{0,2},{1,3},{2,0},{3,1},{4,6},{5,7},{6,4},{7,5},{8,10},{9,11},{10,... | collective-permute-start | bytes 405512 | tf_op jit(solution)/shard_map/ppermute | solution.py:29
  86.4 8.6 %collective-permute-start.33 = (f32[264,128]{1,0:T(8,128)S(1)}, f32[264,128]{1,0:T(8,128)S(1)}, u32[]{:S(2)}, u32[]{:S(2)}) collective-permute-start(f32[264,128]{1,0:T(8,128)S(1)} %get-tuple-element.59), channel_id=1, source_target_pairs={{0,4},{1,5},{2,6},{3,7},{4,0},{5,1},{6,2},{7,3},{8,12},{9,13},{10,... | collective-permute-start | bytes 405512 | tf_op jit(solution)/shard_map/ppermute | solution.py:29
  86.4 8.5 %collective-permute-start.34 = (f32[264,128]{1,0:T(8,128)S(1)}, f32[264,128]{1,0:T(8,128)S(1)}, u32[]{:S(2)}, u32[]{:S(2)}) collective-permute-start(f32[264,128]{1,0:T(8,128)S(1)} %get-tuple-element.60), channel_id=1, source_target_pairs={{0,6},{1,7},{2,4},{3,5},{4,2},{5,3},{6,0},{7,1},{8,14},{9,15},{10,... | collective-permute-start | bytes 405512 | tf_op jit(solution)/shard_map/ppermute | solution.py:29
  (16 other events, 54.4 us)
